TPU v7x, 128 devices: a whole 4x4x4 slice. The times are simulated.
128 devices in a mesh: stream: 16 (over y_lo, z, core), span: 8 (over x, y_hi).
Axes of the slice: x: 4, y: 4 (y_hi: 2, y_lo: 2; y = y_hi * 2 + y_lo), z: 4, core: 2. Of those that a mesh axis runs over, the one named last changes fastest.
Arguments:
- conserved: float32 [5, 32, 256, 512], P(None, 'stream', 'span'), may hold values from -1.1 to 7, as said below
- phase_mask: int32 [32, 256, 512], P('stream', 'span'), may hold values from 0 to 2, as said below
- diag_inverse: float32 [5, 5, 32, 256, 512], P(None, None, 'stream', 'span'), may hold values from -0.25 to 2.9
Outputs:
- update: float32 [5, 32, 256, 512], P(None, 'stream', 'span')
- residual: float32 [5, 32, 256, 512], P(None, 'stream', 'span')
Inputs may be any that keep to these rules, and one draw needn't show every extreme that they name: `phase_mask`: phase region of each cell: 0 liquid, 1 vapor, 2 mixture. `conserved`: each cell holds a stiffened gas of its phase at a pressure of 0.8 to 1.2, every velocity component within 0.15 of zero and a sound speed of 0.7 or more.
All inputs are finite; a program needn't handle non-finite values.
Results may differ from a plain program's by a relative error of at most 0.0003.
Values sent between devices are 32-bit elements; how exact they have to be, the bound alone decides.
A program may use at most 192 MiB of HBM per device.

v0:
```python
import jax
import jax.numpy as jnp
from jax import lax
from jax.sharding import PartitionSpec as P

face_area = 0.0625


def from_behind(array, axis, by):
    devices = lax.axis_size(axis)
    pairs = [(i, i + by) for i in range(devices) if 0 <= i + by < devices]
    return lax.ppermute(array, axis, pairs)


def with_halo(cells, sides, width):
    for axis, dim in sides:
        count = lax.axis_size(axis)
        head = lax.slice_in_dim(cells, 0, width, axis=dim)
        tail = lax.slice_in_dim(cells, cells.shape[dim] - width, cells.shape[dim], axis=dim)
        cells = jnp.concatenate(
            [
                lax.ppermute(tail, axis, [(i, (i + 1) % count) for i in range(count)]),
                cells,
                lax.ppermute(head, axis, [((i + 1) % count, i) for i in range(count)]),
            ],
            axis=dim,
        )
    return cells


def eos_table(phase_mask):
    heat_ratio = jnp.where(phase_mask == 0, 4.4, jnp.where(phase_mask == 1, 1.4, 2.0)).astype(
        jnp.float32
    )
    stiffness = jnp.where(phase_mask == 0, 1.0, jnp.where(phase_mask == 1, 0.0, 0.5)).astype(
        jnp.float32
    )
    return (heat_ratio, stiffness)


def derive(conserved, phase_mask):
    heat_ratio, stiffness = eos_table(phase_mask)
    density = conserved[0]
    speed_flow = conserved[1] / density
    speed_span = conserved[2] / density
    speed_wall = conserved[3] / density
    kinetic = (
        0.5
        * density
        * (speed_flow * speed_flow + speed_span * speed_span + speed_wall * speed_wall)
    )
    pressure = (heat_ratio - 1.0) * (conserved[4] - kinetic) - heat_ratio * stiffness
    acoustic_celerity = jnp.sqrt(heat_ratio * (pressure + stiffness) / density)
    return jnp.concatenate([conserved, pressure[None], acoustic_celerity[None]], axis=0)


def physical(fields, normal, speed):
    pressure = fields[5]
    pieces = [fields[normal]]
    for column in (1, 2, 3):
        adding = fields[column] * speed
        if column == normal:
            adding = adding + pressure
        pieces.append(adding)
    pieces.append((fields[4] + pressure) * speed)
    return pieces


def star_flux(fields, normal, speed, wave, moving, contact, fluxes):
    factor = moving / (wave - contact)
    starred = [factor]
    for column in (1, 2, 3):
        if column == normal:
            starred.append(factor * contact)
        else:
            starred.append(factor * (fields[column] / fields[0]))
    starred.append(
        factor * (fields[4] / fields[0] + (contact - speed) * (contact + fields[5] / moving))
    )
    return [fluxes[column] + wave * (starred[column] - fields[column]) for column in range(5)]


def riemann_flux(left_state, right_state, normal):
    speed_left = left_state[normal] / left_state[0]
    speed_right = right_state[normal] / right_state[0]
    wave_left = jnp.minimum(speed_left - left_state[6], speed_right - right_state[6])
    wave_right = jnp.maximum(speed_left + left_state[6], speed_right + right_state[6])
    mass_left = left_state[0] * (wave_left - speed_left)
    mass_right = right_state[0] * (wave_right - speed_right)
    contact = (
        right_state[5] - left_state[5] + mass_left * speed_left - mass_right * speed_right
    ) / (mass_left - mass_right)
    flux_left = physical(left_state, normal, speed_left)
    flux_right = physical(right_state, normal, speed_right)
    star_left = star_flux(left_state, normal, speed_left, wave_left, mass_left, contact, flux_left)
    star_right = star_flux(
        right_state, normal, speed_right, wave_right, mass_right, contact, flux_right
    )
    chosen = []
    for column in range(5):
        chosen.append(
            jnp.where(
                wave_left >= 0.0,
                flux_left[column],
                jnp.where(
                    contact >= 0.0,
                    star_left[column],
                    jnp.where(wave_right >= 0.0, star_right[column], flux_right[column]),
                ),
            )
        )
    return jnp.stack(chosen)


def block_residual(padded):
    inside = padded[:, 1:-1, 1:-1]
    flux_along = riemann_flux(padded[:, :-1, 1:-1], padded[:, 1:, 1:-1], 1)
    flux_across = riemann_flux(padded[:, 1:-1, :-1], padded[:, 1:-1, 1:], 2)
    neighbour = jnp.concatenate([inside[:, :, :, 1:], inside[:, :, :, -1:]], axis=3)
    flux_normal = riemann_flux(inside, neighbour, 3)
    surface = inside[:, :, :, :1]
    mirror = jnp.concatenate([surface[:3], -surface[3:4], surface[4:]], axis=0)
    flux_wall = riemann_flux(mirror, surface, 3)
    below = jnp.concatenate([flux_wall, flux_normal[:, :, :, :-1]], axis=3)
    return face_area * (
        flux_along[:, 1:]
        - flux_along[:, :-1]
        + (flux_across[:, :, 1:] - flux_across[:, :, :-1])
        + (flux_normal - below)
    )


def apply_block(matrix, vector):
    summed = matrix[:, 0] * vector[0]
    for column in range(1, 5):
        summed = summed + matrix[:, column] * vector[column]
    return summed


def forward(diag_inverse, source, coupling, incoming):
    planes = source.shape[1]

    def advance(plane_at, carried):
        flowing, outputs = carried
        matrix = lax.dynamic_index_in_dim(diag_inverse, plane_at, 2, keepdims=False)
        entry = lax.dynamic_index_in_dim(source, plane_at, 1, keepdims=False)
        result = apply_block(matrix, entry + flowing)
        outputs = lax.dynamic_update_index_in_dim(outputs, result, plane_at, 1)
        weight = lax.dynamic_index_in_dim(coupling, plane_at, 0, keepdims=False)
        return (weight * result, outputs)

    flowing, outputs = lax.fori_loop(0, planes, advance, (incoming, jnp.zeros_like(source)))
    return (outputs, flowing)


def backward(diag_inverse, sweep, coupling, incoming):
    planes = sweep.shape[1]

    def retreat(turn_at, carried):
        flowing, outputs = carried
        plane_at = planes - 1 - turn_at
        matrix = lax.dynamic_index_in_dim(diag_inverse, plane_at, 2, keepdims=False)
        earlier = lax.dynamic_index_in_dim(sweep, plane_at, 1, keepdims=False)
        result = earlier + apply_block(matrix, flowing)
        outputs = lax.dynamic_update_index_in_dim(outputs, result, plane_at, 1)
        weight = lax.dynamic_index_in_dim(coupling, plane_at, 0, keepdims=False)
        return (weight * result, outputs)

    flowing, outputs = lax.fori_loop(0, planes, retreat, (incoming, jnp.zeros_like(sweep)))
    return (outputs, flowing)


def forward_wave(diag_inverse, source, coupling, breadth):
    sections = lax.axis_size("stream")
    position = lax.axis_index("stream")
    segments = source.shape[3] // breadth

    def forward_section_turn(section_at, carried):
        outputs, incoming = carried
        segment = section_at - position
        active = jnp.logical_and(segment >= 0, segment < segments)

        def forward_working(outputs):
            result, outgoing = forward(diag_inverse, source, coupling, incoming)
            return (result, outgoing)

        def forward_resting(outputs):
            return (outputs, jnp.zeros_like(incoming))

        outputs, outgoing = lax.cond(active, forward_working, forward_resting, outputs)
        incoming = from_behind(outgoing, "stream", 1)
        return (outputs, incoming)

    initial = (jnp.zeros_like(source), jnp.zeros((5, source.shape[2], breadth), jnp.float32))
    return lax.fori_loop(0, sections + segments - 1, forward_section_turn, initial)[0]


def backward_wave(diag_inverse, sweep, coupling, breadth):
    sections = lax.axis_size("stream")
    position = sections - 1 - lax.axis_index("stream")
    segments = sweep.shape[3] // breadth

    def backward_section_turn(section_at, carried):
        outputs, incoming = carried
        segment = section_at - position
        active = jnp.logical_and(segment >= 0, segment < segments)

        def backward_working(outputs):
            result, outgoing = backward(diag_inverse, sweep, coupling, incoming)
            return (result, outgoing)

        def backward_resting(outputs):
            return (outputs, jnp.zeros_like(incoming))

        outputs, outgoing = lax.cond(active, backward_working, backward_resting, outputs)
        incoming = from_behind(outgoing, "stream", -1)
        return (outputs, incoming)

    initial = (jnp.zeros_like(sweep), jnp.zeros((5, sweep.shape[2], breadth), jnp.float32))
    return lax.fori_loop(0, sections + segments - 1, backward_section_turn, initial)[0]


def body(conserved, phase_mask, diag_inverse):
    fields = derive(conserved, phase_mask)
    padded = with_halo(fields, (("stream", 1), ("span", 2)), 1)
    planes = fields.shape[1]
    at_inlet = lax.axis_index("stream") == 0
    at_outlet = lax.axis_index("stream") == lax.axis_size("stream") - 1
    ghost_low = jnp.where(at_inlet, padded[:, 1:2], padded[:, 0:1])
    ghost_high = jnp.where(
        at_outlet, padded[:, planes : planes + 1], padded[:, planes + 1 : planes + 2]
    )
    padded = jnp.concatenate([ghost_low, padded[:, 1 : planes + 1], ghost_high], axis=1)
    residual = block_residual(padded)
    coupling = 0.5 * (jnp.abs(fields[1] / fields[0]) + fields[6])
    source = -residual
    breadth = source.shape[3]
    sweep = forward_wave(diag_inverse, source, coupling, breadth)
    update = backward_wave(diag_inverse, sweep, coupling, breadth)
    return (update, residual)


def solution(mesh):
    in_specs = (
        P(None, "stream", "span", None),
        P("stream", "span", None),
        P(None, None, "stream", "span", None),
    )
    out_specs = (P(None, "stream", "span", None), P(None, "stream", "span", None))
    return jax.shard_map(body, mesh=mesh, in_specs=in_specs, out_specs=out_specs, check_vma=False)
```

profile of v0, /device:TPU:1, one launch (start us, length us, event | category | flops | bytes accessed | tf_op | source)
XLA Modules:
  0.0 564.4 jit_solution(10191185468946800225)
XLA Ops:
  48.1 177.6 %while.68 = (s32[]{:T(128)}, f32[5,2,32,512]{3,2,1,0:T(8,128)}, f32[5,32,512]{2,1,0:T(8,128)}, s32[]{:T(128)}, f32[2,32,512]{2,1,0:T(8,128)S(1)}, /*index=5*/f32...) while((s32[]{:T(128)}, f32[5,2,32,512]{3,2,1,0:T(8,128)}, ...), condition=%wide.region_5.6_spmd, body=%wide.region_0.5_spmd.sunk | while | flops 1638409 | bytes 11666292 | solution.py:195
  50.8 9.2 %collective-permute-done.1 = f32[5,32,512]{2,1,0:T(8,128)} collective-permute-done((f32[5,32,512]{2,1,0:T(8,128)}, f32[5,32,512]{2,1,0:T(8,128)}, u32[]{:S(2)}, u32[]{:S(2)}) %collective-permute-start.1) | collective-permute-done | bytes 327712 | tf_op jit(solution)/shard_map/while/body/eval_jaxpr/ppermute | solution.py:12
  60.0 8.2 %conditional.4 = (f32[5,2,32,512]{3,2,1,0:T(8,128)}, f32[5,32,512]{2,1,0:T(8,128)}) conditional(s32[]{:T(128)} %convert_element_type.16, f32[5,2,32,512]{3,2,1,0:T(8,128)} %get-tuple-element.979, (f32[2,32,512]{2,1,0:T(8,128)S(1)}, f32[5,5,2,32,512]{4,3,0,1,2:T(8,128)S(1)}, f32[5,2,32,512]{3,2,0,1:T(8,128)}, f32[5,32,512]{2,1,0:T(8,128)}) %tuple.183), branch_computations={%region_1.1_spmd, %region_2.4_spmd} | conditional | flops 1638402 | bytes 10355369 | solution.py:190
  75.2 11.8 %collective-permute-start.1 = (f32[5,32,512]{2,1,0:T(8,128)}, f32[5,32,512]{2,1,0:T(8,128)}, u32[]{:S(2)}, u32[]{:S(2)}) collective-permute-start(f32[5,32,512]{2,1,0:T(8,128)} %get-tuple-element.879), channel_id=1, source_target_pairs={{0,8},{8,16},{16,24},{24,32},{32,40},{40,48},{48,56},{56,64},{64,7... | collective-permute-start | bytes 983048 | tf_op jit(solution)/shard_map/while/body/eval_jaxpr/ppermute | solution.py:12
  120.5 6.8 %collective-permute-start.1 = (f32[5,32,512]{2,1,0:T(8,128)}, f32[5,32,512]{2,1,0:T(8,128)}, u32[]{:S(2)}, u32[]{:S(2)}) collective-permute-start(f32[5,32,512]{2,1,0:T(8,128)} %get-tuple-element.879), channel_id=1, source_target_pairs={{0,8},{8,16},{16,24},{24,32},{32,40},{40,48},{48,56},{56,64},{64,7... | collective-permute-start | bytes 983048 | tf_op jit(solution)/shard_map/while/body/eval_jaxpr/ppermute | solution.py:12
  200.9 8.9 %collective-permute-start.1 = (f32[5,32,512]{2,1,0:T(8,128)}, f32[5,32,512]{2,1,0:T(8,128)}, u32[]{:S(2)}, u32[]{:S(2)}) collective-permute-start(f32[5,32,512]{2,1,0:T(8,128)} %get-tuple-element.879), channel_id=1, source_target_pairs={{0,8},{8,16},{16,24},{24,32},{32,40},{40,48},{48,56},{56,64},{64,7... | collective-permute-start | bytes 983048 | tf_op jit(solution)/shard_map/while/body/eval_jaxpr/ppermute | solution.py:12
  227.4 337.1 %while.69 = (s32[]{:T(128)}, f32[5,2,32,512]{3,2,1,0:T(8,128)}, f32[5,32,512]{2,1,0:T(8,128)}, s32[]{:T(128)}, f32[2,32,512]{2,1,0:T(8,128)S(1)}, /*index=5*/f32...) while((s32[]{:T(128)}, f32[5,2,32,512]{3,2,1,0:T(8,128)}, ...), condition=%wide.region_11.12_spmd, body=%wide.region_6.11_spmd.sunk | while | flops 1720333 | bytes 11993546 | solution.py:220
  230.0 9.6 %collective-permute-done = f32[5,32,512]{2,1,0:T(8,128)} collective-permute-done((f32[5,32,512]{2,1,0:T(8,128)}, f32[5,32,512]{2,1,0:T(8,128)}, u32[]{:S(2)}, u32[]{:S(2)}) %collective-permute-start) | collective-permute-done | bytes 327712 | tf_op jit(solution)/shard_map/while/body/eval_jaxpr/ppermute | solution.py:12
  242.3 8.8 %collective-permute-done = f32[5,32,512]{2,1,0:T(8,128)} collective-permute-done((f32[5,32,512]{2,1,0:T(8,128)}, f32[5,32,512]{2,1,0:T(8,128)}, u32[]{:S(2)}, u32[]{:S(2)}) %collective-permute-start) | collective-permute-done | bytes 327712 | tf_op jit(solution)/shard_map/while/body/eval_jaxpr/ppermute | solution.py:12
  253.8 9.6 %collective-permute-done = f32[5,32,512]{2,1,0:T(8,128)} collective-permute-done((f32[5,32,512]{2,1,0:T(8,128)}, f32[5,32,512]{2,1,0:T(8,128)}, u32[]{:S(2)}, u32[]{:S(2)}) %collective-permute-start) | collective-permute-done | bytes 327712 | tf_op jit(solution)/shard_map/while/body/eval_jaxpr/ppermute | solution.py:12
  266.1 8.8 %collective-permute-done = f32[5,32,512]{2,1,0:T(8,128)} collective-permute-done((f32[5,32,512]{2,1,0:T(8,128)}, f32[5,32,512]{2,1,0:T(8,128)}, u32[]{:S(2)}, u32[]{:S(2)}) %collective-permute-start) | collective-permute-done | bytes 327712 | tf_op jit(solution)/shard_map/while/body/eval_jaxpr/ppermute | solution.py:12
  277.5 9.6 %collective-permute-done = f32[5,32,512]{2,1,0:T(8,128)} collective-permute-done((f32[5,32,512]{2,1,0:T(8,128)}, f32[5,32,512]{2,1,0:T(8,128)}, u32[]{:S(2)}, u32[]{:S(2)}) %collective-permute-start) | collective-permute-done | bytes 327712 | tf_op jit(solution)/shard_map/while/body/eval_jaxpr/ppermute | solution.py:12
  289.8 8.8 %collective-permute-done = f32[5,32,512]{2,1,0:T(8,128)} collective-permute-done((f32[5,32,512]{2,1,0:T(8,128)}, f32[5,32,512]{2,1,0:T(8,128)}, u32[]{:S(2)}, u32[]{:S(2)}) %collective-permute-start) | collective-permute-done | bytes 327712 | tf_op jit(solution)/shard_map/while/body/eval_jaxpr/ppermute | solution.py:12
  301.3 9.6 %collective-permute-done = f32[5,32,512]{2,1,0:T(8,128)} collective-permute-done((f32[5,32,512]{2,1,0:T(8,128)}, f32[5,32,512]{2,1,0:T(8,128)}, u32[]{:S(2)}, u32[]{:S(2)}) %collective-permute-start) | collective-permute-done | bytes 327712 | tf_op jit(solution)/shard_map/while/body/eval_jaxpr/ppermute | solution.py:12
  313.6 8.9 %collective-permute-done = f32[5,32,512]{2,1,0:T(8,128)} collective-permute-done((f32[5,32,512]{2,1,0:T(8,128)}, f32[5,32,512]{2,1,0:T(8,128)}, u32[]{:S(2)}, u32[]{:S(2)}) %collective-permute-start) | collective-permute-done | bytes 327712 | tf_op jit(solution)/shard_map/while/body/eval_jaxpr/ppermute | solution.py:12
  325.1 8.9 %collective-permute-done = f32[5,32,512]{2,1,0:T(8,128)} collective-permute-done((f32[5,32,512]{2,1,0:T(8,128)}, f32[5,32,512]{2,1,0:T(8,128)}, u32[]{:S(2)}, u32[]{:S(2)}) %collective-permute-start) | collective-permute-done | bytes 327712 | tf_op jit(solution)/shard_map/while/body/eval_jaxpr/ppermute | solution.py:12
  336.7 8.9 %collective-permute-done = f32[5,32,512]{2,1,0:T(8,128)} collective-permute-done((f32[5,32,512]{2,1,0:T(8,128)}, f32[5,32,512]{2,1,0:T(8,128)}, u32[]{:S(2)}, u32[]{:S(2)}) %collective-permute-start) | collective-permute-done | bytes 327712 | tf_op jit(solution)/shard_map/while/body/eval_jaxpr/ppermute | solution.py:12
  348.2 8.9 %collective-permute-done = f32[5,32,512]{2,1,0:T(8,128)} collective-permute-done((f32[5,32,512]{2,1,0:T(8,128)}, f32[5,32,512]{2,1,0:T(8,128)}, u32[]{:S(2)}, u32[]{:S(2)}) %collective-permute-start) | collective-permute-done | bytes 327712 | tf_op jit(solution)/shard_map/while/body/eval_jaxpr/ppermute | solution.py:12
  359.8 8.9 %collective-permute-done = f32[5,32,512]{2,1,0:T(8,128)} collective-permute-done((f32[5,32,512]{2,1,0:T(8,128)}, f32[5,32,512]{2,1,0:T(8,128)}, u32[]{:S(2)}, u32[]{:S(2)}) %collective-permute-start) | collective-permute-done | bytes 327712 | tf_op jit(solution)/shard_map/while/body/eval_jaxpr/ppermute | solution.py:12
  371.4 8.9 %collective-permute-done = f32[5,32,512]{2,1,0:T(8,128)} collective-permute-done((f32[5,32,512]{2,1,0:T(8,128)}, f32[5,32,512]{2,1,0:T(8,128)}, u32[]{:S(2)}, u32[]{:S(2)}) %collective-permute-start) | collective-permute-done | bytes 327712 | tf_op jit(solution)/shard_map/while/body/eval_jaxpr/ppermute | solution.py:12
  382.9 148.4 %collective-permute-done = f32[5,32,512]{2,1,0:T(8,128)} collective-permute-done((f32[5,32,512]{2,1,0:T(8,128)}, f32[5,32,512]{2,1,0:T(8,128)}, u32[]{:S(2)}, u32[]{:S(2)}) %collective-permute-start) | collective-permute-done | bytes 327712 | tf_op jit(solution)/shard_map/while/body/eval_jaxpr/ppermute | solution.py:12
  531.3 12.9 %conditional.5 = (f32[5,2,32,512]{3,2,1,0:T(8,128)}, f32[5,32,512]{2,1,0:T(8,128)}) conditional(s32[]{:T(128)} %convert_element_type.17, f32[5,2,32,512]{3,2,1,0:T(8,128)} %get-tuple-element.1006, (f32[2,32,512]{2,1,0:T(8,128)S(1)}, f32[5,2,32,512]{3,2,1,0:T(8,128)}, f32[5,5,2,32,512]{4,3,0,1,2:T(8,128)S(1)}, f32[5,32,512]{2,1,0:T(8,128)}) %tuple.185), branch_computations={%region_7.7_spmd, %region_8.10_spmd} | conditional | flops 1720326 | bytes 10682623 | solution.py:215
  532.2 10.3 %while.67 = (s32[]{:T(128)}, f32[5,32,512]{2,1,0:T(8,128)}, f32[5,2,32,512]{3,2,1,0:T(8,128)}, f32[2,32,512]{2,1,0:T(8,128)S(1)}, f32[5,2,32,512]{3,2,1,0:T(8,12...) while((s32[]{:T(128)}, f32[5,32,512]{2,1,0:T(8,128)}, ...), condition=%wide.region_10.9_spmd, body=%wide.region_9.8_spmd.sunk | while | flops 1720326 | bytes 9371803 | solution.py:169
  553.6 9.2 %collective-permute-start = (f32[5,32,512]{2,1,0:T(8,128)}, f32[5,32,512]{2,1,0:T(8,128)}, u32[]{:S(2)}, u32[]{:S(2)}) collective-permute-start(f32[5,32,512]{2,1,0:T(8,128)} %get-tuple-element.888), channel_id=1, source_target_pairs={{8,0},{16,8},{24,16},{32,24},{40,32},{48,40},{56,48},{64,56},{72,6... | collective-permute-start | bytes 983048 | tf_op jit(solution)/shard_map/while/body/eval_jaxpr/ppermute | solution.py:12
  (199 shorter events, 279.4 us)
Async XLA Ops:
  14.8 9.6 %collective-permute-start.4 = (f32[7,4,1,512]{3,1,2,0:T(4,128)S(1)}, f32[7,4,1,512]{3,1,2,0:T(4,128)}, u32[]{:S(2)}, u32[]{:S(2)}) collective-permute-start(f32[7,4,1,512]{3,1,2,0:T(4,128)S(1)} %copy.111), channel_id=1, source_target_pairs={{0,1},{1,2},{2,3},{3,4},{4,5},{5,6},{6,7},{7,0},{8,9},{9,10},{10,1... | collective-permute-start | bytes 172040 | tf_op jit(solution)/shard_map/ppermute | solution.py:22
  48.9 11.1 %collective-permute-start.1 = (f32[5,32,512]{2,1,0:T(8,128)}, f32[5,32,512]{2,1,0:T(8,128)}, u32[]{:S(2)}, u32[]{:S(2)}) collective-permute-start(f32[5,32,512]{2,1,0:T(8,128)} %get-tuple-element.879), channel_id=1, source_target_pairs={{0,8},{8,16},{16,24},{24,32},{32,40},{40,48},{48,56},{56,64},{64,7... | collective-permute-start | bytes 983048 | tf_op jit(solution)/shard_map/while/body/eval_jaxpr/ppermute | solution.py:12
  75.2 16.2 %collective-permute-start.1 = (f32[5,32,512]{2,1,0:T(8,128)}, f32[5,32,512]{2,1,0:T(8,128)}, u32[]{:S(2)}, u32[]{:S(2)}) collective-permute-start(f32[5,32,512]{2,1,0:T(8,128)} %get-tuple-element.879), channel_id=1, source_target_pairs={{0,8},{8,16},{16,24},{24,32},{32,40},{40,48},{48,56},{56,64},{64,7... | collective-permute-start | bytes 983048 | tf_op jit(solution)/shard_map/while/body/eval_jaxpr/ppermute | solution.py:12
  92.1 8.7 %collective-permute-start.1 = (f32[5,32,512]{2,1,0:T(8,128)}, f32[5,32,512]{2,1,0:T(8,128)}, u32[]{:S(2)}, u32[]{:S(2)}) collective-permute-start(f32[5,32,512]{2,1,0:T(8,128)} %get-tuple-element.879), channel_id=1, source_target_pairs={{0,8},{8,16},{16,24},{24,32},{32,40},{40,48},{48,56},{56,64},{64,7... | collective-permute-start | bytes 983048 | tf_op jit(solution)/shard_map/while/body/eval_jaxpr/ppermute | solution.py:12
  120.5 11.1 %collective-permute-start.1 = (f32[5,32,512]{2,1,0:T(8,128)}, f32[5,32,512]{2,1,0:T(8,128)}, u32[]{:S(2)}, u32[]{:S(2)}) collective-permute-start(f32[5,32,512]{2,1,0:T(8,128)} %get-tuple-element.879), channel_id=1, source_target_pairs={{0,8},{8,16},{16,24},{24,32},{32,40},{40,48},{48,56},{56,64},{64,7... | collective-permute-start | bytes 983048 | tf_op jit(solution)/shard_map/while/body/eval_jaxpr/ppermute | solution.py:12
  141.8 8.7 %collective-permute-start.1 = (f32[5,32,512]{2,1,0:T(8,128)}, f32[5,32,512]{2,1,0:T(8,128)}, u32[]{:S(2)}, u32[]{:S(2)}) collective-permute-start(f32[5,32,512]{2,1,0:T(8,128)} %get-tuple-element.879), channel_id=1, source_target_pairs={{0,8},{8,16},{16,24},{24,32},{32,40},{40,48},{48,56},{56,64},{64,7... | collective-permute-start | bytes 983048 | tf_op jit(solution)/shard_map/while/body/eval_jaxpr/ppermute | solution.py:12
  160.7 11.1 %collective-permute-start.1 = (f32[5,32,512]{2,1,0:T(8,128)}, f32[5,32,512]{2,1,0:T(8,128)}, u32[]{:S(2)}, u32[]{:S(2)}) collective-permute-start(f32[5,32,512]{2,1,0:T(8,128)} %get-tuple-element.879), channel_id=1, source_target_pairs={{0,8},{8,16},{16,24},{24,32},{32,40},{40,48},{48,56},{56,64},{64,7... | collective-permute-start | bytes 983048 | tf_op jit(solution)/shard_map/while/body/eval_jaxpr/ppermute | solution.py:12
  200.9 13.2 %collective-permute-start.1 = (f32[5,32,512]{2,1,0:T(8,128)}, f32[5,32,512]{2,1,0:T(8,128)}, u32[]{:S(2)}, u32[]{:S(2)}) collective-permute-start(f32[5,32,512]{2,1,0:T(8,128)} %get-tuple-element.879), channel_id=1, source_target_pairs={{0,8},{8,16},{16,24},{24,32},{32,40},{40,48},{48,56},{56,64},{64,7... | collective-permute-start | bytes 983048 | tf_op jit(solution)/shard_map/while/body/eval_jaxpr/ppermute | solution.py:12
  214.9 10.8 %collective-permute-start.1 = (f32[5,32,512]{2,1,0:T(8,128)}, f32[5,32,512]{2,1,0:T(8,128)}, u32[]{:S(2)}, u32[]{:S(2)}) collective-permute-start(f32[5,32,512]{2,1,0:T(8,128)} %get-tuple-element.879), channel_id=1, source_target_pairs={{0,8},{8,16},{16,24},{24,32},{32,40},{40,48},{48,56},{56,64},{64,7... | collective-permute-start | bytes 983048 | tf_op jit(solution)/shard_map/while/body/eval_jaxpr/ppermute | solution.py:12
  228.1 11.6 %collective-permute-start = (f32[5,32,512]{2,1,0:T(8,128)}, f32[5,32,512]{2,1,0:T(8,128)}, u32[]{:S(2)}, u32[]{:S(2)}) collective-permute-start(f32[5,32,512]{2,1,0:T(8,128)} %get-tuple-element.888), channel_id=1, source_target_pairs={{8,0},{16,8},{24,16},{32,24},{40,32},{48,40},{56,48},{64,56},{72,6... | collective-permute-start | bytes 983048 | tf_op jit(solution)/shard_map/while/body/eval_jaxpr/ppermute | solution.py:12
  240.4 10.7 %collective-permute-start = (f32[5,32,512]{2,1,0:T(8,128)}, f32[5,32,512]{2,1,0:T(8,128)}, u32[]{:S(2)}, u32[]{:S(2)}) collective-permute-start(f32[5,32,512]{2,1,0:T(8,128)} %get-tuple-element.888), channel_id=1, source_target_pairs={{8,0},{16,8},{24,16},{32,24},{40,32},{48,40},{56,48},{64,56},{72,6... | collective-permute-start | bytes 983048 | tf_op jit(solution)/shard_map/while/body/eval_jaxpr/ppermute | solution.py:12
  251.9 11.6 %collective-permute-start = (f32[5,32,512]{2,1,0:T(8,128)}, f32[5,32,512]{2,1,0:T(8,128)}, u32[]{:S(2)}, u32[]{:S(2)}) collective-permute-start(f32[5,32,512]{2,1,0:T(8,128)} %get-tuple-element.888), channel_id=1, source_target_pairs={{8,0},{16,8},{24,16},{32,24},{40,32},{48,40},{56,48},{64,56},{72,6... | collective-permute-start | bytes 983048 | tf_op jit(solution)/shard_map/while/body/eval_jaxpr/ppermute | solution.py:12
  264.2 10.7 %collective-permute-start = (f32[5,32,512]{2,1,0:T(8,128)}, f32[5,32,512]{2,1,0:T(8,128)}, u32[]{:S(2)}, u32[]{:S(2)}) collective-permute-start(f32[5,32,512]{2,1,0:T(8,128)} %get-tuple-element.888), channel_id=1, source_target_pairs={{8,0},{16,8},{24,16},{32,24},{40,32},{48,40},{56,48},{64,56},{72,6... | collective-permute-start | bytes 983048 | tf_op jit(solution)/shard_map/while/body/eval_jaxpr/ppermute | solution.py:12
  275.6 11.6 %collective-permute-start = (f32[5,32,512]{2,1,0:T(8,128)}, f32[5,32,512]{2,1,0:T(8,128)}, u32[]{:S(2)}, u32[]{:S(2)}) collective-permute-start(f32[5,32,512]{2,1,0:T(8,128)} %get-tuple-element.888), channel_id=1, source_target_pairs={{8,0},{16,8},{24,16},{32,24},{40,32},{48,40},{56,48},{64,56},{72,6... | collective-permute-start | bytes 983048 | tf_op jit(solution)/shard_map/while/body/eval_jaxpr/ppermute | solution.py:12
  287.9 10.7 %collective-permute-start = (f32[5,32,512]{2,1,0:T(8,128)}, f32[5,32,512]{2,1,0:T(8,128)}, u32[]{:S(2)}, u32[]{:S(2)}) collective-permute-start(f32[5,32,512]{2,1,0:T(8,128)} %get-tuple-element.888), channel_id=1, source_target_pairs={{8,0},{16,8},{24,16},{32,24},{40,32},{48,40},{56,48},{64,56},{72,6... | collective-permute-start | bytes 983048 | tf_op jit(solution)/shard_map/while/body/eval_jaxpr/ppermute | solution.py:12
  299.3 11.6 %collective-permute-start = (f32[5,32,512]{2,1,0:T(8,128)}, f32[5,32,512]{2,1,0:T(8,128)}, u32[]{:S(2)}, u32[]{:S(2)}) collective-permute-start(f32[5,32,512]{2,1,0:T(8,128)} %get-tuple-element.888), channel_id=1, source_target_pairs={{8,0},{16,8},{24,16},{32,24},{40,32},{48,40},{56,48},{64,56},{72,6... | collective-permute-start | bytes 983048 | tf_op jit(solution)/shard_map/while/body/eval_jaxpr/ppermute | solution.py:12
  311.6 10.8 %collective-permute-start = (f32[5,32,512]{2,1,0:T(8,128)}, f32[5,32,512]{2,1,0:T(8,128)}, u32[]{:S(2)}, u32[]{:S(2)}) collective-permute-start(f32[5,32,512]{2,1,0:T(8,128)} %get-tuple-element.888), channel_id=1, source_target_pairs={{8,0},{16,8},{24,16},{32,24},{40,32},{48,40},{56,48},{64,56},{72,6... | collective-permute-start | bytes 983048 | tf_op jit(solution)/shard_map/while/body/eval_jaxpr/ppermute | solution.py:12
  323.2 10.8 %collective-permute-start = (f32[5,32,512]{2,1,0:T(8,128)}, f32[5,32,512]{2,1,0:T(8,128)}, u32[]{:S(2)}, u32[]{:S(2)}) collective-permute-start(f32[5,32,512]{2,1,0:T(8,128)} %get-tuple-element.888), channel_id=1, source_target_pairs={{8,0},{16,8},{24,16},{32,24},{40,32},{48,40},{56,48},{64,56},{72,6... | collective-permute-start | bytes 983048 | tf_op jit(solution)/shard_map/while/body/eval_jaxpr/ppermute | solution.py:12
  334.8 10.8 %collective-permute-start = (f32[5,32,512]{2,1,0:T(8,128)}, f32[5,32,512]{2,1,0:T(8,128)}, u32[]{:S(2)}, u32[]{:S(2)}) collective-permute-start(f32[5,32,512]{2,1,0:T(8,128)} %get-tuple-element.888), channel_id=1, source_target_pairs={{8,0},{16,8},{24,16},{32,24},{40,32},{48,40},{56,48},{64,56},{72,6... | collective-permute-start | bytes 983048 | tf_op jit(solution)/shard_map/while/body/eval_jaxpr/ppermute | solution.py:12
  346.3 10.8 %collective-permute-start = (f32[5,32,512]{2,1,0:T(8,128)}, f32[5,32,512]{2,1,0:T(8,128)}, u32[]{:S(2)}, u32[]{:S(2)}) collective-permute-start(f32[5,32,512]{2,1,0:T(8,128)} %get-tuple-element.888), channel_id=1, source_target_pairs={{8,0},{16,8},{24,16},{32,24},{40,32},{48,40},{56,48},{64,56},{72,6... | collective-permute-start | bytes 983048 | tf_op jit(solution)/shard_map/while/body/eval_jaxpr/ppermute | solution.py:12
  357.9 10.8 %collective-permute-start = (f32[5,32,512]{2,1,0:T(8,128)}, f32[5,32,512]{2,1,0:T(8,128)}, u32[]{:S(2)}, u32[]{:S(2)}) collective-permute-start(f32[5,32,512]{2,1,0:T(8,128)} %get-tuple-element.888), channel_id=1, source_target_pairs={{8,0},{16,8},{24,16},{32,24},{40,32},{48,40},{56,48},{64,56},{72,6... | collective-permute-start | bytes 983048 | tf_op jit(solution)/shard_map/while/body/eval_jaxpr/ppermute | solution.py:12
  369.4 10.8 %collective-permute-start = (f32[5,32,512]{2,1,0:T(8,128)}, f32[5,32,512]{2,1,0:T(8,128)}, u32[]{:S(2)}, u32[]{:S(2)}) collective-permute-start(f32[5,32,512]{2,1,0:T(8,128)} %get-tuple-element.888), channel_id=1, source_target_pairs={{8,0},{16,8},{24,16},{32,24},{40,32},{48,40},{56,48},{64,56},{72,6... | collective-permute-start | bytes 983048 | tf_op jit(solution)/shard_map/while/body/eval_jaxpr/ppermute | solution.py:12
  381.0 150.3 %collective-permute-start = (f32[5,32,512]{2,1,0:T(8,128)}, f32[5,32,512]{2,1,0:T(8,128)}, u32[]{:S(2)}, u32[]{:S(2)}) collective-permute-start(f32[5,32,512]{2,1,0:T(8,128)} %get-tuple-element.888), channel_id=1, source_target_pairs={{8,0},{16,8},{24,16},{32,24},{40,32},{48,40},{56,48},{64,56},{72,6... | collective-permute-start | bytes 983048 | tf_op jit(solution)/shard_map/while/body/eval_jaxpr/ppermute | solution.py:12
  553.6 10.8 %collective-permute-start = (f32[5,32,512]{2,1,0:T(8,128)}, f32[5,32,512]{2,1,0:T(8,128)}, u32[]{:S(2)}, u32[]{:S(2)}) collective-permute-start(f32[5,32,512]{2,1,0:T(8,128)} %get-tuple-element.888), channel_id=1, source_target_pairs={{8,0},{16,8},{24,16},{32,24},{40,32},{48,40},{56,48},{64,56},{72,6... | collective-permute-start | bytes 983048 | tf_op jit(solution)/shard_map/while/body/eval_jaxpr/ppermute | solution.py:12
  (19 other events, 117.2 us)
where the time goes:
time: 566 us; the launch traced here: 564 us
  waiting for transfers between devices  355 us (63%)
  starting transfers between devices  131 us (23%)
  local copies, waits for them, and re-layouts  42.7 us (8%)
  other arithmetic  34.1 us (6%)
    ppermute x32, waiting for transfers between devices, from_behind(): return lax.ppermute(array, axis, pairs)  349 us
    ppermute x32, starting transfers between devices, from_behind(): return lax.ppermute(array, axis, pairs)  122 us
    another operation x35, local copies, waits for them, and re-layouts  26.8 us
  transfers between devices with their start and end apart: 36, of which 34 were waited for; matrix products, arithmetic and copies ran while one was open for 1% of the time, Pallas kernels for 0%

commit v1 on v0

v1 whole, which is shorter than its diff:
```python
import jax
import jax.numpy as jnp
from jax import lax
from jax.experimental import pallas as pl
from jax.experimental.pallas import tpu as pltpu
from jax.sharding import PartitionSpec as P

face_area = 0.0625
MESH = pl.DeviceIdType.MESH
CHIPS = 8
SOLVER = 1
f32 = jnp.float32


def xor_chip(chip, k):
    return (
        ((k // 4 + chip // 4) % 2) * 4 + ((k // 2 + chip // 2) % 2) * 2 + (k + chip) % 2
    )


def eos(phase):
    ratio = jnp.where(phase == 0, 4.4, jnp.where(phase == 1, 1.4, 2.0)).astype(f32)
    stiff = jnp.where(phase == 0, 1.0, jnp.where(phase == 1, 0.0, 0.5)).astype(f32)
    return ratio, stiff


def primitives(cons, phase):
    ratio, stiff = eos(phase)
    density = cons[0]
    inverse = 1.0 / density
    u1, u2, u3 = cons[1] * inverse, cons[2] * inverse, cons[3] * inverse
    kinetic = 0.5 * density * (u1 * u1 + u2 * u2 + u3 * u3)
    pressure = (ratio - 1.0) * (cons[4] - kinetic) - ratio * stiff
    sound = jnp.sqrt(ratio * (pressure + stiff) * inverse)
    return [density, u1, u2, u3, cons[4] * inverse, pressure, sound]


def hllc(left, right, normal):
    ql, qr = left[normal], right[normal]
    cl, cr = left[6], right[6]
    sl = jnp.minimum(ql - cl, qr - cr)
    sr = jnp.maximum(ql + cl, qr + cr)
    ml = left[0] * (sl - ql)
    mr = right[0] * (sr - qr)
    contact = (right[5] - left[5] + ml * ql - mr * qr) / (ml - mr)
    supersonic = sl >= 0.0
    ahead = contact >= 0.0
    use_left = jnp.logical_or(supersonic, ahead)
    starred = jnp.logical_and(
        jnp.logical_not(supersonic), jnp.logical_or(ahead, sr >= 0.0)
    )
    pick = lambda a, b: jnp.where(use_left, a, b)
    s, m, q = pick(sl, sr), pick(ml, mr), pick(ql, qr)
    p, e = pick(left[5], right[5]), pick(left[4], right[4])
    ss = jnp.where(starred, contact, q)
    inv = 1.0 / (s - ss)
    mass = m * inv * ss
    out = [mass]
    for d in (1, 2, 3):
        if d == normal:
            out.append(s * mass - q * m + p)
        else:
            out.append(pick(left[d], right[d]) * mass)
    out.append(p * q + e * mass + s * (ss - q) * (mass + p * inv))
    return out


def matvec(mat, vec):
    return [
        mat(i, 0) * vec[0]
        + mat(i, 1) * vec[1]
        + mat(i, 2) * vec[2]
        + mat(i, 3) * vec[3]
        + mat(i, 4) * vec[4]
        for i in range(5)
    ]


def kernel(
    cons, phase, diag, upd, resid,
    qp, pp, qg, pg, eq, ep, row_out, row_in, dv, prim, acc, swp, res, upv,
    m_out, n_out, m_all, n_all,
    g_out, g_all, f_out, f_all, h_out, h_all, w_out, w_all,
    loc_sem, chip_send, chip_recv, halo_send, halo_recv, row_send, row_recv,
    m_send, m_recv, n_send, n_recv, g_send, g_recv, f_send, f_recv,
    h_send, h_recv, w_send, w_recv, out_sem, out_send, out_recv,
):
    stream = lax.axis_index("stream")
    span = lax.axis_index("span")
    spans = lax.axis_size("span")
    core = stream % 2
    chip = stream // 2
    other = 1 - core
    span_up = (span + 1) % spans
    span_down = (span + spans - 1) % spans

    def dev(chip_at, core_at, span_at=None):
        return {
            "stream": chip_at * 2 + core_at,
            "span": span if span_at is None else span_at,
        }

    def remote(src, dst, send, recv, device):
        return pltpu.make_async_remote_copy(
            src_ref=src, dst_ref=dst, send_sem=send, recv_sem=recv,
            device_id=device, device_id_type=MESH,
        )

    barrier = pltpu.get_barrier_semaphore()

    def greet(device):
        pl.semaphore_signal(barrier, inc=1, device_id=device, device_id_type=MESH)

    @pl.loop(1, 16)
    def _(step):
        pl.semaphore_signal(
            barrier, inc=1,
            device_id={"stream": (stream + step) % 16, "span": span},
            device_id_type=MESH,
        )

    span_near = core * span_up + other * span_down
    span_far = core * span_down + other * span_up
    greet(dev(chip, core, span_near))
    greet(dev(chip, other, span_near))
    greet(dev(chip, core, span_far))

    mine = pl.ds(2 * core, 2)
    src_rows = pl.ds(pl.multiple_of(8 * core, 8), 24)
    dst_rows = pl.ds(pl.multiple_of(8 * other, 8), 24)
    edge_rows = pl.ds(pl.multiple_of(24 * other, 8), 8)
    half = pl.ds(pl.multiple_of(16 * core, 8), 16)
    other_half = pl.ds(pl.multiple_of(16 * other, 8), 16)
    loads = [
        pltpu.make_async_copy(cons.at[:, :, src_rows], qp.at[:, mine, dst_rows], loc_sem.at[0]),
        pltpu.make_async_copy(phase.at[:, src_rows], pp.at[mine, dst_rows], loc_sem.at[1]),
        pltpu.make_async_copy(cons.at[:, :, edge_rows], eq, loc_sem.at[2]),
        pltpu.make_async_copy(phase.at[:, edge_rows], ep, loc_sem.at[3]),
        pltpu.make_async_copy(diag.at[:, :, :, half], dv.at[:, :, mine], loc_sem.at[4]),
    ]
    for copy in loads:
        copy.start()

    for copy in loads[:4]:
        copy.wait()

    def pack_row(side, cell, phase_cell):
        for ch in range(5):
            for plane in range(2):
                row_out[side, pl.ds(ch * 2 + plane, 1), :] = cell(ch, plane)
        for plane in range(2):
            row_out[side, pl.ds(10 + plane, 1), :] = phase_cell(plane).astype(f32)
        row_out[side, pl.ds(12, 4), :] = jnp.zeros((4, 512), f32)

    @pl.when(core == 0)
    def _():
        pack_row(0, lambda c, p: eq[c, p, pl.ds(7, 1), :], lambda p: ep[p, pl.ds(7, 1), :])
        pack_row(1, lambda c, p: qp[c, p, pl.ds(8, 1), :], lambda p: pp[p, pl.ds(8, 1), :])

    @pl.when(core == 1)
    def _():
        pack_row(0, lambda c, p: qp[c, 2 + p, pl.ds(23, 1), :], lambda p: pp[2 + p, pl.ds(23, 1), :])
        pack_row(1, lambda c, p: eq[c, p, pl.ds(0, 1), :], lambda p: ep[p, pl.ds(0, 1), :])

    pl.semaphore_wait(barrier, 18)

    def halo(core_at):
        rows = pl.ds(16 * core_at, 16)
        return [
            remote(cons.at[:, core, rows], qg.at[other], halo_send.at[core_at, 0],
                   halo_recv.at[other, 0], dev(chip + 2 * core - 1, core_at)),
            remote(phase.at[core, rows], pg.at[other], halo_send.at[core_at, 1],
                   halo_recv.at[other, 1], dev(chip + 2 * core - 1, core_at)),
        ]

    sends_halo = jnp.where(core == 0, chip > 0, chip < CHIPS - 1)

    @pl.when(sends_halo)
    def _():
        for core_at in range(2):
            for copy in halo(core_at):
                copy.start()

    peer = dev(chip, other)
    peer_rows = pl.ds(pl.multiple_of(8 * other, 8), 24)
    peer_dst = pl.ds(pl.multiple_of(8 * core, 8), 24)
    theirs = pl.ds(2 * other, 2)
    swaps = [
        remote(cons.at[:, :, peer_rows], qp.at[:, mine, peer_dst], chip_send.at[0], chip_recv.at[0], peer),
        remote(phase.at[:, peer_rows], pp.at[mine, peer_dst], chip_send.at[1], chip_recv.at[1], peer),
        remote(diag.at[:, :, :, other_half], dv.at[:, :, mine], chip_send.at[2], chip_recv.at[2], peer),
    ]
    swaps[0].start()
    swaps[1].start()
    row_copies = [
        remote(row_out.at[0], row_in.at[core], row_send.at[0], row_recv.at[core], dev(chip, 0, span_up)),
        remote(row_out.at[1], row_in.at[core], row_send.at[1], row_recv.at[core], dev(chip, 1, span_down)),
    ]
    for copy in row_copies:
        copy.start()
    swaps[2].start()

    swaps[0].wait_recv()
    swaps[1].wait_recv()
    for core_at in range(2):
        remote(row_out.at[0], row_in.at[core_at], row_send.at[0], row_recv.at[core_at], peer).wait_recv()
    ghost_row = 7 + 17 * core
    for core_at in range(2):
        for plane in range(2):
            for ch in range(5):
                qp[ch, 2 * core_at + plane, pl.ds(ghost_row, 1), :] = row_in[
                    core_at, pl.ds(ch * 2 + plane, 1), :
                ]
            pp[2 * core_at + plane, pl.ds(ghost_row, 1), :] = row_in[
                core_at, pl.ds(10 + plane, 1), :
            ].astype(jnp.int32)

    @pl.loop(0, 16)
    def _(step):
        plane = step // 4
        rows = pl.ds(pl.multiple_of((step % 4) * 8, 8), 8)
        fields = primitives([qp[ch, plane, rows, :] for ch in range(5)], pp[plane, rows, :])
        for ch in range(7):
            prim[ch, plane + 1, rows, :] = fields[ch]
        prim[7, plane + 1, rows, :] = 0.5 * (jnp.abs(fields[1]) + fields[6])

    def tile(q):
        return (
            pl.ds(pl.multiple_of((q // 4) * 8, 8), 8),
            pl.ds(pl.multiple_of((q % 4) * 128, 128), 128),
        )

    def weight(plane, q):
        return prim[
            7, plane + 1,
            pl.ds(pl.multiple_of((q // 4) * 8 + 8, 8), 8),
            pl.ds(pl.multiple_of((q % 4) * 128, 128), 128),
        ]

    def block(plane, q):
        rows, lanes = tile(q)
        return lambda i, j: dv[i, j, plane, rows, lanes]

    is_solver = core == SOLVER

    loads[4].wait()
    swaps[2].wait_recv()

    def chip_product(q, order):
        prod = None
        for plane in order:
            mat = block(plane, q)
            w = weight(plane, q)
            if prod is None:
                prod = [[mat(i, j) * w for j in range(5)] for i in range(5)]
            else:
                cols = [
                    matvec(mat, [prod[i][j] for i in range(5)]) for j in range(5)
                ]
                prod = [[cols[j][i] * w for j in range(5)] for i in range(5)]
        return prod

    inner = jnp.logical_and(chip > 0, chip < CHIPS - 1)

    def send_products(out, gathered, send, recv, order):
        @pl.loop(0, CHIPS)
        def _(step):
            q = xor_chip(chip, CHIPS - 1 - step)
            prod = chip_product(q, order)
            for i in range(5):
                for j in range(5):
                    out[q, i, j] = prod[i][j]
            to_self = jnp.logical_and(is_solver, q == chip)

            @pl.when(jnp.logical_not(to_self))
            def _():
                remote(out.at[q], gathered.at[core, chip], send.at[q], recv.at[core, chip],
                       dev(q, SOLVER)).start()

            @pl.when(to_self)
            def _():
                gathered[core, chip] = out[q]

    @pl.when(inner)
    def _():
        send_products(m_out, m_all, m_send, m_recv, (0, 1, 2, 3))

    lane = lax.broadcasted_iota(jnp.int32, (8, 512), 1)

    @pl.loop(0, 8)
    def _(step):
        plane = step // 2
        rows = pl.ds(pl.multiple_of((step % 2) * 8 + 8, 8), 8)
        out_rows = pl.ds(pl.multiple_of((step % 2) * 8, 8), 8)
        cell = [prim[ch, plane + 1, rows, :] for ch in range(7)]
        below = []
        for ch in range(7):
            first = -cell[ch] if ch == 3 else cell[ch]
            below.append(jnp.where(lane == 0, first, pltpu.roll(cell[ch], 1, axis=1)))
        low = hllc(below, cell, 3)
        mass = cell[0] * cell[3]
        top = [
            mass, cell[1] * mass, cell[2] * mass, cell[3] * mass + cell[5],
            cell[4] * mass + cell[5] * cell[3],
        ]
        for ch in range(5):
            high = jnp.where(lane == 511, top[ch], pltpu.roll(low[ch], 511, axis=1))
            acc[ch, plane, out_rows, :] = high - low[ch]

    @pl.loop(0, 16)
    def _(step):
        plane = step // 4
        lanes = pl.ds(pl.multiple_of((step % 4) * 128, 128), 128)
        down = [prim[ch, plane + 1, pl.ds(7, 24), lanes] for ch in range(7)]
        cell = [prim[ch, plane + 1, pl.ds(8, 24), lanes] for ch in range(7)]
        low = hllc(down, cell, 2)
        for ch in range(5):
            high = pltpu.roll(low[ch], 23, axis=0)
            acc[ch, plane, :, lanes] = acc[ch, plane, :, lanes] + (high - low[ch])[:16]

    @pl.when(chip == 0)
    def _():
        for ch in range(7):
            prim[ch, 0, pl.ds(8, 16), :] = prim[ch, 1, pl.ds(8, 16), :]

    @pl.when(chip == CHIPS - 1)
    def _():
        for ch in range(7):
            prim[ch, 5, pl.ds(8, 16), :] = prim[ch, 4, pl.ds(8, 16), :]

    def take_halo(side):
        remote(cons.at[:, 0, pl.ds(0, 16)], qg.at[side], halo_send.at[0, 0], halo_recv.at[side, 0], peer).wait_recv()
        remote(phase.at[0, pl.ds(0, 16)], pg.at[side], halo_send.at[0, 1], halo_recv.at[side, 1], peer).wait_recv()

        @pl.loop(0, 2)
        def _(part):
            rows = pl.ds(pl.multiple_of(part * 8, 8), 8)
            fields = primitives([qg[side, ch, rows, :] for ch in range(5)], pg[side, rows, :])
            for ch in range(7):
                prim[ch, 5 * side, pl.ds(pl.multiple_of(part * 8 + 8, 8), 8), :] = fields[ch]

    @pl.when(chip > 0)
    def _():
        take_halo(0)

    @pl.when(chip < CHIPS - 1)
    def _():
        take_halo(1)

    @pl.loop(0, CHIPS)
    def _(step):
        q = xor_chip(chip, CHIPS - 1 - step)
        rows, lanes = tile(q)
        prim_rows = pl.ds(pl.multiple_of((q // 4) * 8 + 8, 8), 8)
        states = lambda plane: [prim[ch, plane, prim_rows, lanes] for ch in range(7)]
        low = hllc(states(0), states(1), 1)
        flow = None
        for plane in range(4):
            high = hllc(states(plane + 1), states(plane + 2), 1)
            entry = []
            for ch in range(5):
                value = face_area * (acc[ch, plane, rows, lanes] + (high[ch] - low[ch]))
                res[ch, plane, rows, lanes] = value
                entry.append(-value if flow is None else flow[ch] - value)
            low = high
            w = weight(plane, q)
            flow = [w * value for value in matvec(block(plane, q), entry)]

        for ch in range(5):
            g_out[q, ch] = flow[ch]
        to_self = jnp.logical_and(is_solver, q == chip)

        @pl.when(jnp.logical_and(jnp.logical_not(to_self), chip < CHIPS - 1))
        def _():
            remote(g_out.at[q], g_all.at[core, chip], g_send.at[q], g_recv.at[core, chip],
                   dev(q, SOLVER)).start()

        @pl.when(to_self)
        def _():
            g_all[core, chip] = g_out[q]

    out_copies = [
        pltpu.make_async_copy(res.at[:, mine], resid.at[:, :, half], out_sem.at[0]),
        remote(res.at[:, theirs], resid.at[:, :, half], out_send.at[0], out_recv.at[0], peer),
    ]
    for copy in out_copies:
        copy.start()

    @pl.when(inner)
    def _():
        send_products(n_out, n_all, n_send, n_recv, (3, 2, 1, 0))

    def gather_wait(gathered, recv, src_chip):
        for src_core in range(2):
            def wait():
                remote(gathered.at[src_core, src_chip], gathered.at[src_core, src_chip],
                       recv.at[src_core, src_chip], recv.at[src_core, src_chip], peer).wait_recv()

            if src_core == SOLVER:
                pl.when(chip != src_chip)(wait)
            else:
                wait()

    def scatter(values, out, landed, send, recv, to_chip):
        for to_core in range(2):
            for ch in range(5):
                out[to_core, to_chip, ch] = values[to_core][ch]

            def start():
                remote(out.at[to_core, to_chip], landed.at[chip], send.at[to_core, to_chip],
                       recv.at[chip], dev(to_chip, to_core)).start()

            if to_core == SOLVER:
                pl.when(chip != to_chip)(start)

                @pl.when(chip == to_chip)
                def _():
                    for ch in range(5):
                        landed[chip, ch] = values[to_core][ch]
            else:
                start()

    def recurrence(mats, mats_recv, vecs, vecs_recv, out, landed, send, recv, order):
        flow = None
        for at, src in enumerate(order[:-1]):
            gather_wait(vecs, vecs_recv, src)
            new = []
            if at > 0:
                gather_wait(mats, mats_recv, src)
            for a in range(2):
                value = [vecs[a, src, ch] for ch in range(5)]
                if at > 0:
                    moved = matvec(lambda i, j: mats[a, src, i, j], flow[a])
                    value = [x + y for x, y in zip(value, moved)]
                new.append(value)
            flow = new
            scatter(flow, out, landed, send, recv, order[at + 1])

    @pl.when(is_solver)
    def _():
        recurrence(m_all, m_recv, g_all, g_recv, f_out, f_all, f_send, f_recv, tuple(range(CHIPS)))

    def landed_wait(landed, recv, q):
        @pl.when(jnp.logical_not(jnp.logical_and(is_solver, q == chip)))
        def _():
            remote(landed.at[q], landed.at[q], recv.at[q], recv.at[q], peer).wait_recv()

    @pl.when(chip == 0)
    def _():
        f_all[...] = jnp.zeros_like(f_all)

    @pl.loop(0, CHIPS)
    def _(step):
        q = xor_chip(chip, step)
        rows, lanes = tile(q)

        @pl.when(chip > 0)
        def _():
            landed_wait(f_all, f_recv, q)

        flow = [f_all[q, ch] for ch in range(5)]
        sweep = []
        for plane in range(4):
            entry = [flow[ch] - res[ch, plane, rows, lanes] for ch in range(5)]
            value = matvec(block(plane, q), entry)
            sweep.append(value)
            for ch in range(5):
                swp[ch, plane, rows, lanes] = value[ch]
            w = weight(plane, q)
            flow = [w * x for x in value]
        for plane in (2, 1, 0):
            moved = matvec(block(plane, q), flow)
            w = weight(plane, q)
            flow = [w * (x + y) for x, y in zip(sweep[plane], moved)]
        for ch in range(5):
            h_out[q, ch] = flow[ch]
        to_self = jnp.logical_and(is_solver, q == chip)

        @pl.when(jnp.logical_and(jnp.logical_not(to_self), chip > 0))
        def _():
            remote(h_out.at[q], h_all.at[core, chip], h_send.at[q], h_recv.at[core, chip],
                   dev(q, SOLVER)).start()

        @pl.when(to_self)
        def _():
            h_all[core, chip] = h_out[q]

    @pl.when(is_solver)
    def _():
        recurrence(n_all, n_recv, h_all, h_recv, w_out, w_all, w_send, w_recv,
                   tuple(range(CHIPS - 1, -1, -1)))

    @pl.when(chip == CHIPS - 1)
    def _():
        w_all[...] = jnp.zeros_like(w_all)

    @pl.loop(0, CHIPS)
    def _(step):
        q = xor_chip(chip, step)
        rows, lanes = tile(q)

        @pl.when(chip < CHIPS - 1)
        def _():
            landed_wait(w_all, w_recv, q)

        flow = [w_all[q, ch] for ch in range(5)]
        for plane in (3, 2, 1, 0):
            moved = matvec(block(plane, q), flow)
            value = [swp[ch, plane, rows, lanes] + moved[ch] for ch in range(5)]
            for ch in range(5):
                upv[ch, plane, rows, lanes] = value[ch]
            w = weight(plane, q)
            flow = [w * x for x in value]

    final = [
        pltpu.make_async_copy(upv.at[:, mine], upd.at[:, :, half], out_sem.at[1]),
        remote(upv.at[:, theirs], upd.at[:, :, half], out_send.at[1], out_recv.at[1], peer),
    ]
    for copy in final:
        copy.start()

    for copy in swaps:
        copy.wait_send()
    for copy in row_copies:
        copy.wait_send()

    @pl.when(sends_halo)
    def _():
        for core_at in range(2):
            for copy in halo(core_at):
                copy.wait_send()

    @pl.loop(0, CHIPS)
    def _(q):
        not_self = jnp.logical_not(jnp.logical_and(is_solver, q == chip))

        def drain(out, gathered, send, recv, when):
            @pl.when(jnp.logical_and(not_self, when))
            def _():
                remote(out.at[q], gathered.at[core, chip], send.at[q], recv.at[core, chip], peer).wait_send()

        drain(m_out, m_all, m_send, m_recv, inner)
        drain(n_out, n_all, n_send, n_recv, inner)
        drain(g_out, g_all, g_send, g_recv, chip < CHIPS - 1)
        drain(h_out, h_all, h_send, h_recv, chip > 0)

    @pl.when(is_solver)
    def _():
        def drain(out, landed, send, recv, to_chip):
            for to_core in range(2):
                def wait():
                    remote(out.at[to_core, to_chip], landed.at[chip], send.at[to_core, to_chip],
                           recv.at[chip], peer).wait_send()

                if to_core == SOLVER:
                    pl.when(chip != to_chip)(wait)
                else:
                    wait()

        for to_chip in range(1, CHIPS):
            drain(f_out, f_all, f_send, f_recv, to_chip)
        for to_chip in range(CHIPS - 1):
            drain(w_out, w_all, w_send, w_recv, to_chip)

    out_copies[0].wait()
    out_copies[1].wait()
    final[0].wait()
    final[1].wait()


def body(cons, phase, diag):
    dma = pltpu.SemaphoreType.DMA
    vm = lambda *shape: pltpu.VMEM(shape, f32)
    vi = lambda *shape: pltpu.VMEM(shape, jnp.int32)
    per_chip = lambda *shape: vm(CHIPS, *shape, 8, 128)
    scratch = [
        vm(5, 4, 32, 512), vi(4, 32, 512), vm(2, 5, 16, 512), vi(2, 16, 512),
        vm(5, 2, 8, 512), vi(2, 8, 512), vm(2, 16, 512), vm(2, 16, 512),
        vm(5, 5, 4, 16, 512), vm(8, 6, 32, 512),
        vm(5, 4, 16, 512), vm(5, 4, 16, 512), vm(5, 4, 16, 512), vm(5, 4, 16, 512),
        per_chip(5, 5), per_chip(5, 5), vm(2, CHIPS, 5, 5, 8, 128), vm(2, CHIPS, 5, 5, 8, 128),
        per_chip(5), vm(2, CHIPS, 5, 8, 128), vm(2, CHIPS, 5, 8, 128), per_chip(5),
        per_chip(5), vm(2, CHIPS, 5, 8, 128), vm(2, CHIPS, 5, 8, 128), per_chip(5),
        dma((5,)), dma((3,)), dma((3,)), dma((2, 2)), dma((2, 2)), dma((2,)), dma((2,)),
        dma((CHIPS,)), dma((2, CHIPS)), dma((CHIPS,)), dma((2, CHIPS)),
        dma((CHIPS,)), dma((2, CHIPS)), dma((2, CHIPS)), dma((CHIPS,)),
        dma((CHIPS,)), dma((2, CHIPS)), dma((2, CHIPS)), dma((CHIPS,)),
        dma((2,)), dma((2,)), dma((2,)),
    ]
    out = jax.ShapeDtypeStruct(cons.shape, f32)
    anywhere = pl.BlockSpec(memory_space=pl.ANY)
    return pl.pallas_call(
        kernel,
        out_shape=(out, out),
        in_specs=[anywhere] * 3,
        out_specs=(anywhere, anywhere),
        scratch_shapes=scratch,
        compiler_params=pltpu.CompilerParams(
            collective_id=0, has_side_effects=True, vmem_limit_bytes=40 * 2**20
        ),
        name="flow_sweep",
    )(cons, phase, diag)


def solution(mesh):
    in_specs = (
        P(None, "stream", "span", None),
        P("stream", "span", None),
        P(None, None, "stream", "span", None),
    )
    out_specs = (P(None, "stream", "span", None), P(None, "stream", "span", None))
    return jax.shard_map(body, mesh=mesh, in_specs=in_specs, out_specs=out_specs, check_vma=False)
```

time: 566 us -> 56.5 us (0.10)
  waiting for transfers between devices: 355 us -> 0 us
  starting transfers between devices: 131 us -> 0 us
  Pallas kernels: 0 us -> 50.1 us
  local copies, waits for them, and re-layouts: 42.7 us -> 5.58 us
  other arithmetic: 34.1 us -> 0 us
    ppermute x36 -> x0, waiting for transfers between devices: 355 us -> none  [the longest x32 349 us: from_behind(): return lax.ppermute(array, axis, pairs)]
    ppermute x36 -> x0, starting transfers between devices: 131 us -> none  [the longest x32 122 us: from_behind(): return lax.ppermute(array, axis, pairs)]
    pallas_call x0 -> x1, Pallas kernels: none -> 50.1 us  [body(): pl.pallas_call(kernel, out_shape=(out, out), in_specs=[anywhere] * 3, out...]
    another operation x36 -> x0, local copies, waits for them, and re-layouts: 26.8 us -> none
    select_n x4 -> x0, other arithmetic: 10.5 us -> none  [the longest x3 9.34 us: riemann_flux(): jnp.where(wave_left >= 0.0, flux_left[column], jnp.where(contact >= 0.0,...]
    mul x5 -> x0, other arithmetic: 7.22 us -> none  [the longest x2 3.97 us: retreat(): return (weight * result, outputs)]
    dynamic_update_slice x4 -> x0, other arithmetic: 5.84 us -> none  [the longest x2 3.94 us: retreat(): outputs = lax.dynamic_update_index_in_dim(outputs, result, plane_at, 1)]
  transfers between devices with their start and end apart: 36 -> 0, of which waited for: 34 -> 0; matrix products, arithmetic and copies ran while one was open for 1% -> 0% of each run, Pallas kernels for 0% -> 0%
where the time goes in v1:
time: 56.5 us; the launch traced here: 56.3 us
  Pallas kernels  50.1 us (89%)
  local copies, waits for them, and re-layouts  5.58 us (10%)
  between operations  0.65 us (1%)
    pallas_call x1, Pallas kernels, body(): pl.pallas_call(kernel, out_shape=(out, out), in_specs=[anywhere] * 3, out...  50.1 us
    unnamed x8, local copies, waits for them, and re-layouts  5.58 us

profile of v1, /device:TPU:1, one launch (start us, length us, event | category | flops | bytes accessed | tf_op | source)
XLA Modules:
  0.0 56.3 jit_solution(8399199922331924424)
XLA Ops:
  0.6 0.0 copy-start
  0.6 1.9 %copy-done = f32[5,5,2,32,512]{4,3,2,1,0:T(8,128)S(1)} copy-done((f32[5,5,2,32,512]{4,3,2,1,0:T(8,128)S(1)}, f32[5,5,2,32,512]{4,3,2,1,0:T(8,128)}, u32[]{:S(2)}) %copy-start) | copy-done | bytes 3276824
  2.6 0.0 copy-start.1
  2.6 1.1 %copy-done.1 = f32[5,2,32,512]{3,2,1,0:T(8,128)S(1)} copy-done((f32[5,2,32,512]{3,2,1,0:T(8,128)S(1)}, f32[5,2,32,512]{3,2,1,0:T(8,128)}, u32[]{:S(2)}) %copy-start.1) | copy-done | bytes 655384
  3.6 0.0 copy-start.2
  3.6 0.9 %copy-done.2 = s32[2,32,512]{2,1,0:T(8,128)S(1)} copy-done((s32[2,32,512]{2,1,0:T(8,128)S(1)}, s32[2,32,512]{2,1,0:T(8,128)}, u32[]{:S(2)}) %copy-start.2) | copy-done | bytes 131096
  4.5 50.1 %flow_sweep.1 = (f32[5,2,32,512]{3,2,1,0:T(8,128)S(1)}, f32[5,2,32,512]{3,2,1,0:T(8,128)S(1)}) custom-call(f32[5,2,32,512]{3,2,1,0:T(8,128)S(1)} %copy-done.1, s32[2,32,512]{2,1,0:T(8,128)S(1)} %copy-done.2, f32[5,5,2,32,512]{4,3,2,1,0:T(8,128)S(1)} %copy-done), custom_call_target="tpu_custom_call" | custom-call | tf_op jit(solution)/shard_map/flow_sweep/pallas_call | solution.py:592
  54.6 0.8 %copy.7 = f32[5,2,32,512]{3,2,1,0:T(8,128)} copy(f32[5,2,32,512]{3,2,1,0:T(8,128)S(1)} %get-tuple-element.4) | data formatting | bytes 1310720
  55.5 0.8 %copy.8 = f32[5,2,32,512]{3,2,1,0:T(8,128)} copy(f32[5,2,32,512]{3,2,1,0:T(8,128)S(1)} %get-tuple-element.5) | data formatting | bytes 1310720
Async XLA Ops:
  0.6 1.9 %copy-start = (f32[5,5,2,32,512]{4,3,2,1,0:T(8,128)S(1)}, f32[5,5,2,32,512]{4,3,2,1,0:T(8,128)}, u32[]{:S(2)}) copy-start(f32[5,5,2,32,512]{4,3,2,1,0:T(8,128)} %diag.1) | copy-start | bytes 9830404
  2.6 1.1 %copy-start.1 = (f32[5,2,32,512]{3,2,1,0:T(8,128)S(1)}, f32[5,2,32,512]{3,2,1,0:T(8,128)}, u32[]{:S(2)}) copy-start(f32[5,2,32,512]{3,2,1,0:T(8,128)} %cons.1) | copy-start | bytes 1966084
  3.6 0.9 %copy-start.2 = (s32[2,32,512]{2,1,0:T(8,128)S(1)}, s32[2,32,512]{2,1,0:T(8,128)}, u32[]{:S(2)}) copy-start(s32[2,32,512]{2,1,0:T(8,128)} %phase.1) | copy-start | bytes 393220

commit v2 on v1

v2 whole, which is shorter than its diff:
```python
import jax
import jax.numpy as jnp
from jax import lax
from jax.experimental import pallas as pl
from jax.experimental.pallas import tpu as pltpu
from jax.sharding import PartitionSpec as P

face_area = 0.0625
MESH = pl.DeviceIdType.MESH
CHIPS = 8
SOLVER = 1
f32 = jnp.float32


def eos(phase):
    ratio = jnp.where(phase == 0, 4.4, jnp.where(phase == 1, 1.4, 2.0)).astype(f32)
    stiff = jnp.where(phase == 0, 1.0, jnp.where(phase == 1, 0.0, 0.5)).astype(f32)
    return ratio, stiff


def primitives(cons, phase):
    ratio, stiff = eos(phase)
    density = cons[0]
    inverse = 1.0 / density
    u1, u2, u3 = cons[1] * inverse, cons[2] * inverse, cons[3] * inverse
    kinetic = 0.5 * density * (u1 * u1 + u2 * u2 + u3 * u3)
    pressure = (ratio - 1.0) * (cons[4] - kinetic) - ratio * stiff
    sound = jnp.sqrt(ratio * (pressure + stiff) * inverse)
    return [density, u1, u2, u3, cons[4] * inverse, pressure, sound]


def hllc(left, right, normal):
    ql, qr = left[normal], right[normal]
    cl, cr = left[6], right[6]
    sl = jnp.minimum(ql - cl, qr - cr)
    sr = jnp.maximum(ql + cl, qr + cr)
    ml = left[0] * (sl - ql)
    mr = right[0] * (sr - qr)
    contact = (right[5] - left[5] + ml * ql - mr * qr) / (ml - mr)
    supersonic = sl >= 0.0
    ahead = contact >= 0.0
    use_left = jnp.logical_or(supersonic, ahead)
    starred = jnp.logical_and(
        jnp.logical_not(supersonic), jnp.logical_or(ahead, sr >= 0.0)
    )
    pick = lambda a, b: jnp.where(use_left, a, b)
    s, m, q = pick(sl, sr), pick(ml, mr), pick(ql, qr)
    p, e = pick(left[5], right[5]), pick(left[4], right[4])
    ss = jnp.where(starred, contact, q)
    inv = 1.0 / (s - ss)
    mass = m * inv * ss
    out = [mass]
    for d in (1, 2, 3):
        if d == normal:
            out.append(s * mass - q * m + p)
        else:
            out.append(pick(left[d], right[d]) * mass)
    out.append(p * q + e * mass + s * (ss - q) * (mass + p * inv))
    return out


def matvec(mat, vec):
    return [
        mat(i, 0) * vec[0]
        + mat(i, 1) * vec[1]
        + mat(i, 2) * vec[2]
        + mat(i, 3) * vec[3]
        + mat(i, 4) * vec[4]
        for i in range(5)
    ]


def kernel(
    cons, phase, diag, upd, resid,
    qo, po, qp, pp, qg, pg, row_out, row_in, wo, do, dv, prim, acc, swp, res, upv, hloc,
    mx, nx, pm, pn, km, m_out, n_out, m_all, n_all,
    g_out, g_all, f_out, f_all, h_out, h_all, w_out, w_all,
    loc_sem, chip_send, chip_recv, mx_recv, halo_send, halo_recv, row_send, row_recv,
    sent, nx_recv, m_recv, n_recv, g_recv, h_recv, f_recv, w_recv, out_sem, out_send, out_recv,
):
    stream = lax.axis_index("stream")
    span = lax.axis_index("span")
    spans = lax.axis_size("span")
    core = stream % 2
    chip = stream // 2
    other = 1 - core
    bits = (chip // 4, (chip // 2) % 2, chip % 2)
    span_up = (span + 1) % spans
    span_down = (span + spans - 1) % spans
    is_solver = core == SOLVER
    mx_send, nx_send, m_send, n_send, g_send, h_send, f_send, w_send = [sent.at[k] for k in range(8)]
    inner = jnp.logical_and(chip > 0, chip < CHIPS - 1)

    def dev(chip_at, core_at, span_at=None):
        return {
            "stream": chip_at * 2 + core_at,
            "span": span if span_at is None else span_at,
        }

    def remote(src, dst, send, recv, device):
        return pltpu.make_async_remote_copy(
            src_ref=src, dst_ref=dst, send_sem=send, recv_sem=recv,
            device_id=device, device_id_type=MESH,
        )

    def flip(bit, by):
        return bit + by - 2 * bit * by

    def aligned(value, by):
        return pl.multiple_of(value, by)

    def each_chip(run, near_first=False, halves=(0, 1), quarters=(0, 1)):
        turn = (lambda i: i) if near_first else (lambda i: 1 - i)

        @pl.loop(halves[0], halves[-1] + 1)
        def _(a):
            rb = flip(bits[0], turn(a))

            @pl.loop(quarters[0], quarters[-1] + 1)
            def _(b):
                l2 = flip(bits[1], turn(b))

                @pl.loop(0, 2)
                def _(c):
                    lb = l2 * 2 + flip(bits[2], turn(c))
                    run(rb * 4 + lb, rb, lb)

    peer = dev(chip, other)

    mine = pl.ds(2 * core, 2)
    theirs = pl.ds(2 * other, 2)
    half = pl.ds(aligned(16 * core, 16), 16)
    other_half = pl.ds(aligned(16 * other, 16), 16)
    loads = [
        pltpu.make_async_copy(cons, qo, loc_sem.at[0]),
        pltpu.make_async_copy(phase, po, loc_sem.at[1]),
        pltpu.make_async_copy(diag.at[:, :, :, other_half], do, loc_sem.at[2]),
        pltpu.make_async_copy(diag.at[:, :, :, half], dv.at[:, :, mine], loc_sem.at[3]),
        pltpu.make_async_copy(
            cons.at[:, :, pl.ds(aligned(8 * core, 8), 24)],
            qp.at[:, mine, pl.ds(aligned(8 * other, 8), 24)], loc_sem.at[4]),
        pltpu.make_async_copy(
            phase.at[:, pl.ds(aligned(8 * core, 8), 24)],
            pp.at[mine, pl.ds(aligned(8 * other, 8), 24)], loc_sem.at[5]),
    ]
    for copy in loads:
        copy.start()

    barrier = pltpu.get_barrier_semaphore()

    def greet(device):
        pl.semaphore_signal(barrier, inc=1, device_id=device, device_id_type=MESH)

    span_near = core * span_up + other * span_down
    span_far = core * span_down + other * span_up
    greet(dev(chip, core, span_near))
    greet(dev(chip, other, span_near))
    greet(dev(chip, core, span_far))
    for k in range(7, -1, -1):
        at = [flip(bits[n], (k >> (2 - n)) & 1) for n in range(3)]
        to = at[0] * 4 + at[1] * 2 + at[2]
        greet(dev(to, other))
        if k:
            greet(dev(to, core))

    loads[0].wait()
    loads[1].wait()
    for side, at in ((0, 31), (1, 0)):
        for ch in range(5):
            for plane in range(2):
                row_out[side, pl.ds(ch * 2 + plane, 1), :] = qo[ch, plane, pl.ds(at, 1), :]
        for plane in range(2):
            row_out[side, pl.ds(10 + plane, 1), :] = po[plane, pl.ds(at, 1), :].astype(f32)
        row_out[side, pl.ds(12, 4), :] = jnp.zeros((4, 512), f32)

    @pl.loop(0, 2)
    def _(plane):
        @pl.loop(0, 4)
        def _(part):
            rows = pl.ds(aligned(part * 8, 8), 8)
            fields = primitives([qo[ch, plane, rows, :] for ch in range(5)], po[plane, rows, :])
            wo[plane, rows, :] = 0.5 * (jnp.abs(fields[1]) + fields[6])

    def weighted(mat, w):
        return [[mat(i, j) * w for j in range(5)] for i in range(5)]

    def product(mat, right, w=None):
        cols = [matvec(mat, [right[i][j] for i in range(5)]) for j in range(5)]
        return [[cols[j][i] if w is None else cols[j][i] * w for j in range(5)] for i in range(5)]

    def put(ref, at, prod):
        for i in range(5):
            for j in range(5):
                ref[(*at, i, j)] = prod[i][j]

    def own_products(half_at, mat_of, m_at, n_at):
        def run(q, rb, lb):
            rows = pl.ds(aligned(rb * 8, 8), 8)
            lanes = pl.ds(aligned(lb * 128, 128), 128)
            w_rows = pl.ds(aligned(half_at * 16 + rb * 8, 8), 8)
            w = [wo[plane, w_rows, lanes] for plane in range(2)]
            mats = [
                (lambda i, j, plane=plane: mat_of(i, j, plane, rows, lanes)) for plane in range(2)
            ]
            put(m_at[0], (*m_at[1], q), product(mats[1], weighted(mats[0], w[0]), w[1]))
            put(n_at[0], (*n_at[1], q), product(mats[0], weighted(mats[1], w[1]), w[0]))

        each_chip(run)

    loads[2].wait()
    own_products(other, lambda i, j, p, r, l: do[i, j, p, r, l], (mx, ()), (nx, ()))
    loads[3].wait()
    own_products(core, lambda i, j, p, r, l: dv[i, j, 2 * core + p, r, l], (pm, (core,)), (pn, (core,)))
    loads[4].wait()
    loads[5].wait()

    pl.semaphore_wait(barrier, 18)

    ahead = chip + 2 * core - 1

    def halo(core_at, part):
        rb = flip(bits[0], 1 - part)
        src = pl.ds(aligned(16 * core_at + 8 * rb, 8), 8)
        dst = pl.ds(aligned(8 * rb, 8), 8)
        return [
            remote(qo.at[:, core, src], qg.at[other, :, dst], halo_send.at[0],
                   halo_recv.at[other, rb, 0], dev(ahead, core_at)),
            remote(po.at[core, src], pg.at[other, dst], halo_send.at[1],
                   halo_recv.at[other, rb, 1], dev(ahead, core_at)),
        ]

    sends_halo = jnp.logical_or(
        jnp.logical_and(core == 0, chip > 0), jnp.logical_and(core == 1, chip < CHIPS - 1)
    )


    peer_rows = pl.ds(aligned(8 * other, 8), 24)
    peer_dst = pl.ds(aligned(8 * core, 8), 24)
    swaps = [
        remote(qo.at[:, :, peer_rows], qp.at[:, mine, peer_dst], chip_send.at[0], chip_recv.at[0], peer),
        remote(po.at[:, peer_rows], pp.at[mine, peer_dst], chip_send.at[1], chip_recv.at[1], peer),
        remote(do, dv.at[:, :, mine], chip_send.at[2], chip_recv.at[2], peer),
    ]
    row_copies = [
        remote(row_out.at[0], row_in.at[core], row_send.at[0], row_recv.at[core], dev(chip, 0, span_up)),
        remote(row_out.at[1], row_in.at[core], row_send.at[1], row_recv.at[core], dev(chip, 1, span_down)),
    ]

    def mx_copy(q):
        return remote(mx.at[q], pm.at[core, q], mx_send, mx_recv.at[q], peer)

    def nx_copy():
        return remote(nx, pn.at[core], nx_send, nx_recv.at[0], peer)

    for copy in row_copies:
        copy.start()

    @pl.when(sends_halo)
    def _():
        for part in range(2):
            for core_at in range(2):
                for copy in halo(core_at, part):
                    copy.start()

    @pl.when(inner)
    def _():
        each_chip(lambda q, rb, lb: mx_copy(q).start())

    swaps[0].start()
    swaps[1].start()

    def slot(core_at, chip_at):
        return core_at * CHIPS + chip_at

    def to_solver(q, out, gathered, send, recv, when=None):
        to_self = jnp.logical_and(is_solver, q == chip)
        goes = jnp.logical_not(to_self)

        @pl.when(goes if when is None else jnp.logical_and(goes, when))
        def _():
            remote(out.at[q], gathered.at[slot(core, chip)], send, recv.at[0], dev(q, SOLVER)).start()

        @pl.when(to_self)
        def _():
            gathered[slot(core, chip)] = out[q]

    def chip_product(parts, left, right, out, q):
        mat = lambda i, j: parts[left, q, i, j]
        right_mat = [[parts[right, q, i, j] for j in range(5)] for i in range(5)]
        put(out, (q,), product(mat, right_mat))

    @pl.when(inner)
    def _():
        def run(q, rb, lb):
            mx_copy(q).wait_recv()
            chip_product(pm, 1, 0, m_out, q)
            to_solver(q, m_out, m_all, m_send, m_recv)

        each_chip(run)
        nx_copy().start()

    swaps[2].start()

    def send_n(half_at, quarters=(0, 1)):
        def run(q, rb, lb):
            chip_product(pn, 0, 1, n_out, q)
            to_solver(q, n_out, n_all, n_send, n_recv)

        @pl.when(inner)
        def _():
            each_chip(run, halves=(half_at,), quarters=quarters)

    def set_primitives(plane, first):
        rows = pl.ds(aligned(first, 8), 8)
        fields = primitives([qp[ch, plane, rows, :] for ch in range(5)], pp[plane, rows, :])
        for ch in range(7):
            prim[ch, plane + 1, rows, :] = fields[ch]
        prim[7, plane + 1, rows, :] = 0.5 * (jnp.abs(fields[1]) + fields[6])

    swaps[0].wait_recv()
    swaps[1].wait_recv()

    @pl.loop(0, 4)
    def _(plane):
        @pl.loop(0, 3)
        def _(part):
            set_primitives(plane, 8 * (other + part))

    lane = lax.broadcasted_iota(jnp.int32, (8, 512), 1)

    @pl.loop(0, 4)
    def _(plane):
        @pl.loop(0, 2)
        def _(part):
            rows = pl.ds(aligned(part * 8 + 8, 8), 8)
            out_rows = pl.ds(aligned(part * 8, 8), 8)
            cell = [prim[ch, plane + 1, rows, :] for ch in range(7)]
            below = []
            for ch in range(7):
                first = -cell[ch] if ch == 3 else cell[ch]
                below.append(jnp.where(lane == 0, first, pltpu.roll(cell[ch], 1, axis=1)))
            low = hllc(below, cell, 3)
            mass = cell[0] * cell[3]
            top = [
                mass, cell[1] * mass, cell[2] * mass, cell[3] * mass + cell[5],
                cell[4] * mass + cell[5] * cell[3],
            ]
            for ch in range(5):
                high = jnp.where(lane == 511, top[ch], pltpu.roll(low[ch], 511, axis=1))
                acc[ch, plane, out_rows, :] = high - low[ch]

    @pl.loop(0, 2)
    def _(part):
        rows = pl.ds(aligned(part * 8 + 8, 8), 8)
        out_rows = pl.ds(aligned(part * 8, 8), 8)

        @pl.loop(0, 3)
        def _(plane):
            states = lambda p: [prim[ch, p, rows, :] for ch in range(7)]
            face = hllc(states(plane + 1), states(plane + 2), 1)
            for ch in range(5):
                acc[ch, plane, out_rows, :] = acc[ch, plane, out_rows, :] + face[ch]
                acc[ch, plane + 1, out_rows, :] = acc[ch, plane + 1, out_rows, :] - face[ch]

    for core_at in range(2):
        remote(row_out.at[0], row_in.at[core_at], row_send.at[0], row_recv.at[core_at], peer).wait_recv()
    ghost_row = 7 + 17 * core
    for core_at in range(2):
        for plane in range(2):
            for ch in range(5):
                qp[ch, 2 * core_at + plane, pl.ds(ghost_row, 1), :] = row_in[
                    core_at, pl.ds(ch * 2 + plane, 1), :
                ]
            pp[2 * core_at + plane, pl.ds(ghost_row, 1), :] = row_in[
                core_at, pl.ds(10 + plane, 1), :
            ].astype(jnp.int32)

    @pl.loop(0, 4)
    def _(plane):
        set_primitives(plane, 24 * core)

    @pl.loop(0, 4)
    def _(plane):
        @pl.loop(0, 4)
        def _(part):
            lanes = pl.ds(aligned(part * 128, 128), 128)
            down = [prim[ch, plane + 1, pl.ds(7, 24), lanes] for ch in range(7)]
            cell = [prim[ch, plane + 1, pl.ds(8, 24), lanes] for ch in range(7)]
            low = hllc(down, cell, 2)
            for ch in range(5):
                high = pltpu.roll(low[ch], 23, axis=0)
                acc[ch, plane, :, lanes] = acc[ch, plane, :, lanes] + (high - low[ch])[:16]

    def block(plane, rb, lb):
        rows = pl.ds(aligned(rb * 8, 8), 8)
        lanes = pl.ds(aligned(lb * 128, 128), 128)
        return lambda i, j: dv[i, j, plane, rows, lanes]

    def weight(plane, rb, lb):
        return prim[7, plane + 1, pl.ds(aligned(rb * 8 + 8, 8), 8), pl.ds(aligned(lb * 128, 128), 128)]

    def cells(ref, plane, rb, lb):
        rows = pl.ds(aligned(rb * 8, 8), 8)
        lanes = pl.ds(aligned(lb * 128, 128), 128)
        return [ref[ch, plane, rows, lanes] for ch in range(5)]

    def set_cells(ref, plane, rb, lb, values):
        rows = pl.ds(aligned(rb * 8, 8), 8)
        lanes = pl.ds(aligned(lb * 128, 128), 128)
        for ch in range(5):
            ref[ch, plane, rows, lanes] = values[ch]

    def edge_face(side, rb):
        rows = pl.ds(aligned(rb * 8 + 8, 8), 8)
        out_rows = pl.ds(aligned(rb * 8, 8), 8)
        inside = [prim[ch, 1 + 3 * side, rows, :] for ch in range(7)]

        def add(outside):
            face = hllc(outside, inside, 1) if side == 0 else hllc(inside, outside, 1)
            for ch in range(5):
                value = acc[ch, 3 * side, out_rows, :]
                acc[ch, 3 * side, out_rows, :] = value - face[ch] if side == 0 else value + face[ch]

        at_end = chip == (CHIPS - 1) * side

        @pl.when(at_end)
        def _():
            add(inside)

        @pl.when(jnp.logical_not(at_end))
        def _():
            dst = pl.ds(aligned(rb * 8, 8), 8)
            remote(qg.at[side, :, dst], qg.at[side, :, dst], halo_send.at[0],
                   halo_recv.at[side, rb, 0], peer).wait_recv()
            remote(pg.at[side, dst], pg.at[side, dst], halo_send.at[1],
                   halo_recv.at[side, rb, 1], peer).wait_recv()
            add(primitives([qg[side, ch, dst, :] for ch in range(5)], pg[side, dst, :]))

    swaps[2].wait_recv()

    for group in range(2):
        rb_at = flip(bits[0], 1 - group)
        for side in range(2):
            edge_face(side, rb_at)

        def local_forward(q, rb, lb):
            flow = None
            for plane in range(4):
                value = [face_area * x for x in cells(acc, plane, rb, lb)]
                set_cells(res, plane, rb, lb, value)
                entry = [-x for x in value] if flow is None else [y - x for x, y in zip(value, flow)]
                value = matvec(block(plane, rb, lb), entry)
                set_cells(swp, plane, rb, lb, value)
                w = weight(plane, rb, lb)
                flow = [w * x for x in value]
            for ch in range(5):
                g_out[q, ch] = flow[ch]
            to_solver(q, g_out, g_all, g_send, g_recv, chip < CHIPS - 1)

        each_chip(local_forward, halves=(group,))

    @pl.when(inner)
    def _():
        nx_copy().wait_recv()

    send_n(0, (0,))

    def response(q, rb, lb):
        blocks = [block(plane, rb, lb) for plane in range(4)]
        ws = [weight(plane, rb, lb) for plane in range(4)]

        def back(sweep):
            flow = [ws[3] * x for x in sweep[3]]
            for plane in (2, 1, 0):
                moved = matvec(blocks[plane], flow)
                flow = [ws[plane] * (x + y) for x, y in zip(sweep[plane], moved)]
            return flow

        local = back([cells(swp, plane, rb, lb) for plane in range(4)])
        for ch in range(5):
            hloc[q, ch] = local[ch]
        for j in range(5):
            sweep = [[blocks[0](i, j) for i in range(5)]]
            for plane in range(1, 4):
                sweep.append(matvec(blocks[plane], [ws[plane - 1] * x for x in sweep[-1]]))
            column = back(sweep)
            for i in range(5):
                km[q, i, j] = column[i]

    each_chip(response)

    def gather_wait(gathered, recv, total, fewer):
        @pl.when(fewer)
        def _():
            part = gathered.at[pl.ds(0, total - 1)]
            remote(part, part, sent.at[8], recv.at[0], peer).wait_recv()

        @pl.when(jnp.logical_not(fewer))
        def _():
            part = gathered.at[pl.ds(0, total)]
            remote(part, part, sent.at[8], recv.at[0], peer).wait_recv()

    def scatter(values, out, landed, send, recv, to_chip):
        for to_core in range(2):
            at = slot(to_core, to_chip)
            for ch in range(5):
                out[at, ch] = values[to_core][ch]

            def start():
                remote(out.at[at], landed.at[chip], send, recv.at[bits[0]], dev(to_chip, to_core)).start()

            if to_core == SOLVER:
                pl.when(chip != to_chip)(start)

                @pl.when(chip == to_chip)
                def _():
                    for ch in range(5):
                        landed[chip, ch] = values[to_core][ch]
            else:
                start()

    def recurrence(mats, vecs, out, landed, send, recv, order):
        flow = None
        for at, src in enumerate(order[:-1]):
            new = []
            for a in range(2):
                value = [vecs[slot(a, src), ch] for ch in range(5)]
                if at > 0:
                    moved = matvec(lambda i, j: mats[slot(a, src), i, j], flow[a])
                    value = [x + y for x, y in zip(value, moved)]
                new.append(value)
            flow = new
            scatter(flow, out, landed, send, recv, order[at + 1])

    @pl.when(is_solver)
    def _():
        gather_wait(m_all, m_recv, 2 * (CHIPS - 2), inner)
        gather_wait(g_all, g_recv, 2 * (CHIPS - 1), chip < CHIPS - 1)
        recurrence(m_all, g_all, f_out, f_all, f_send, f_recv, tuple(range(CHIPS)))
        send_n(0, (1,))
        send_n(1, (0,))


    def landed_wait(landed, recv, rb):
        fewer = jnp.logical_and(is_solver, rb == bits[0])

        @pl.when(fewer)
        def _():
            part = landed.at[pl.ds(0, 3)]
            remote(part, part, sent.at[8], recv.at[rb], peer).wait_recv()

        @pl.when(jnp.logical_not(fewer))
        def _():
            part = landed.at[pl.ds(0, 4)]
            remote(part, part, sent.at[8], recv.at[rb], peer).wait_recv()

    @pl.when(chip == 0)
    def _():
        f_all[...] = jnp.zeros_like(f_all)

    def backward_start(q, rb, lb):
        moved = matvec(lambda i, j: km[q, i, j], [f_all[q, ch] for ch in range(5)])
        for ch in range(5):
            h_out[q, ch] = hloc[q, ch] + moved[ch]
        to_solver(q, h_out, h_all, h_send, h_recv, chip > 0)

    for group in range(2):
        @pl.when(chip > 0)
        def _():
            landed_wait(f_all, f_recv, flip(bits[0], group))

        each_chip(backward_start, near_first=True, halves=(group,))

    @pl.when(jnp.logical_not(is_solver))
    def _():
        send_n(0, (1,))
        send_n(1, (0,))

    send_n(1, (1,))

    out_copies = [
        pltpu.make_async_copy(res.at[:, mine], resid.at[:, :, half], out_sem.at[0]),
        remote(res.at[:, theirs], resid.at[:, :, half], out_send.at[0], out_recv.at[0], peer),
    ]
    for copy in out_copies:
        copy.start()

    def both_sweeps(q, rb, lb):
        flow = [f_all[q, ch] for ch in range(5)]
        sweep = []
        for plane in range(4):
            entry = [y - x for x, y in zip(cells(res, plane, rb, lb), flow)]
            sweep.append(matvec(block(plane, rb, lb), entry))
            w = weight(plane, rb, lb)
            flow = [w * x for x in sweep[-1]]
        value = sweep[3]
        set_cells(swp, 3, rb, lb, value)
        for plane in (2, 1, 0):
            w = weight(plane + 1, rb, lb)
            moved = matvec(block(plane, rb, lb), [w * x for x in value])
            value = [x + y for x, y in zip(sweep[plane], moved)]
            set_cells(swp, plane, rb, lb, value)

    each_chip(both_sweeps)

    @pl.when(is_solver)
    def _():
        gather_wait(n_all, n_recv, 2 * (CHIPS - 2), inner)
        gather_wait(h_all, h_recv, 2 * (CHIPS - 1), chip > 0)
        recurrence(n_all, h_all, w_out, w_all, w_send, w_recv, tuple(range(CHIPS - 1, -1, -1)))

    @pl.when(chip == CHIPS - 1)
    def _():
        w_all[...] = jnp.zeros_like(w_all)

    def finish(q, rb, lb):
        flow = [w_all[q, ch] for ch in range(5)]
        for plane in (3, 2, 1, 0):
            moved = matvec(block(plane, rb, lb), flow)
            set_cells(upv, plane, rb, lb, [x + y for x, y in zip(cells(swp, plane, rb, lb), moved)])
            w = weight(plane, rb, lb)
            flow = [w * x for x in moved]

    def final(group):
        rb = flip(bits[0], group)
        src = pl.ds(aligned(8 * rb, 8), 8)
        dst = pl.ds(aligned(16 * core + 8 * rb, 8), 8)
        return [
            remote(upv.at[:, theirs, src], upd.at[:, :, dst], out_send.at[1 + group],
                   out_recv.at[1 + group], peer),
            pltpu.make_async_copy(upv.at[:, mine, src], upd.at[:, :, dst], out_sem.at[1 + group]),
        ]

    for group in range(2):
        @pl.when(chip < CHIPS - 1)
        def _():
            landed_wait(w_all, w_recv, flip(bits[0], group))

        each_chip(finish, near_first=True, halves=(group,))
        for copy in final(group):
            copy.start()

    for copy in swaps:
        copy.wait_send()
    for copy in row_copies:
        copy.wait_send()

    def drain(part, send):
        remote(part, part, send, nx_recv.at[0], peer).wait_send()

    @pl.when(sends_halo)
    def _():
        drain(qo.at[:, 0], halo_send.at[0])
        drain(po.at[0], halo_send.at[1])

    def drain_either(out, send, total, fewer, when):
        for less in (False, True):
            case = fewer if less else jnp.logical_not(fewer)

            @pl.when(case if when is None else jnp.logical_and(case, when))
            def _():
                drain(out.at[pl.ds(0, total - less)], send)

    @pl.when(inner)
    def _():
        drain(mx, mx_send)
        drain(nx, nx_send)

    drain_either(m_out, m_send, CHIPS, is_solver, inner)
    drain_either(n_out, n_send, CHIPS, is_solver, inner)
    drain_either(g_out, g_send, CHIPS, is_solver, chip < CHIPS - 1)
    drain_either(h_out, h_send, CHIPS, is_solver, chip > 0)
    drain_either(f_out, f_send, 2 * (CHIPS - 1), chip > 0, is_solver)
    drain_either(w_out, w_send, 2 * (CHIPS - 1), chip < CHIPS - 1, is_solver)

    out_copies[0].wait()
    out_copies[1].wait()
    for group in range(2):
        for copy in final(group):
            copy.wait()


def body(cons, phase, diag):
    dma = pltpu.SemaphoreType.DMA
    vm = lambda *shape: pltpu.VMEM(shape, f32)
    vi = lambda *shape: pltpu.VMEM(shape, jnp.int32)
    vecs = lambda *lead: vm(*lead, CHIPS, 5, 8, 128)
    mats = lambda *lead: vm(*lead, CHIPS, 5, 5, 8, 128)
    vecs2, mats2 = vm(2 * CHIPS, 5, 8, 128), vm(2 * CHIPS, 5, 5, 8, 128)
    scratch = [
        vm(5, 2, 32, 512), vi(2, 32, 512), vm(5, 4, 32, 512), vi(4, 32, 512),
        vm(2, 5, 16, 512), vi(2, 16, 512), vm(2, 16, 512), vm(2, 16, 512), vm(2, 32, 512),
        vm(5, 5, 2, 16, 512), vm(5, 5, 4, 16, 512), vm(8, 5, 32, 512),
        vm(5, 4, 16, 512), vm(5, 4, 16, 512), vm(5, 4, 16, 512), vm(5, 4, 16, 512), vecs(),
        mats(), mats(), mats(2), mats(2), mats(), mats(), mats(), mats2, mats2,
        vecs(), vecs2, vecs2, vecs(), vecs(), vecs2, vecs2, vecs(),
        dma((6,)), dma((3,)), dma((3,)), dma((CHIPS,)), dma((2,)), dma((2, 2, 2)), dma((2,)), dma((2,)),
        dma((9,)), dma((1,)), dma((1,)), dma((1,)), dma((1,)), dma((1,)), dma((2,)), dma((2,)),
        dma((3,)), dma((3,)), dma((3,)),
    ]
    out = jax.ShapeDtypeStruct(cons.shape, f32)
    anywhere = pl.BlockSpec(memory_space=pl.ANY)
    hbm = pl.BlockSpec(memory_space=pltpu.HBM)
    return pl.pallas_call(
        kernel,
        out_shape=(out, out),
        in_specs=[hbm] * 3,
        out_specs=(anywhere, anywhere),
        scratch_shapes=scratch,
        compiler_params=pltpu.CompilerParams(
            collective_id=0, has_side_effects=True, vmem_limit_bytes=60 * 2**20
        ),
        name="flow_sweep",
    )(cons, phase, diag)

def solution(mesh):
    in_specs = (
        P(None, "stream", "span", None),
        P("stream", "span", None),
        P(None, None, "stream", "span", None),
    )
    out_specs = (P(None, "stream", "span", None), P(None, "stream", "span", None))
    return jax.shard_map(body, mesh=mesh, in_specs=in_specs, out_specs=out_specs, check_vma=False)
```

time: 56.5 us -> 53.4 us (0.945)
  local copies, waits for them, and re-layouts: 5.58 us -> 3.93 us
  Pallas kernels: 50.1 us -> 48.6 us
    unnamed x8 -> x2, local copies, waits for them, and re-layouts: 5.58 us -> 3.93 us
    pallas_call x1, Pallas kernels: 50.1 us -> 48.6 us  [body(): pl.pallas_call(kernel, out_shape=(out, out), in_specs=[hbm] * 3, out_spec...]
where the time goes in v2:
time: 53.4 us; the launch traced here: 53.2 us
  Pallas kernels  48.6 us (91%)
  local copies, waits for them, and re-layouts  3.93 us (7%)
  between operations  0.64 us (1%)
    pallas_call x1, Pallas kernels, body(): pl.pallas_call(kernel, out_shape=(out, out), in_specs=[hbm] * 3, out_spec...  48.6 us
    unnamed x2, local copies, waits for them, and re-layouts  3.93 us

profile of v2, /device:TPU:1, one launch (start us, length us, event | category | flops | bytes accessed | tf_op | source)
XLA Modules:
  0.0 53.2 jit_solution(11516385370301925221)
XLA Ops:
  0.6 48.6 %flow_sweep.1 = (f32[5,2,32,512]{3,2,1,0:T(8,128)}, f32[5,2,32,512]{3,2,1,0:T(8,128)}) custom-call(f32[5,2,32,512]{3,2,1,0:T(8,128)} %cons.1, s32[2,32,512]{2,1,0:T(8,128)} %phase.1, f32[5,5,2,32,512]{4,3,2,1,0:T(8,128)} %diag.1), custom_call_target="tpu_custom_call" | custom-call | tf_op jit(solution)/shard_map/flow_sweep/pallas_call | solution.py:704
  49.3 2.0 %copy.7 = f32[5,2,32,512]{3,2,1,0:T(8,128)} copy(f32[5,2,32,512]{3,2,1,0:T(8,128)} %get-tuple-element.4) | data formatting | bytes 1310720
  51.2 2.0 %copy.8 = f32[5,2,32,512]{3,2,1,0:T(8,128)} copy(f32[5,2,32,512]{3,2,1,0:T(8,128)} %get-tuple-element.5) | data formatting | bytes 1310720

commit v3 on v2

--- a/solution.py
+++ b/solution.py
@@ -463,7 +463,6 @@
     def _():
         nx_copy().wait_recv()
 
-    send_n(0, (0,))
 
     def response(q, rb, lb):
         blocks = [block(plane, rb, lb) for plane in range(4)]
@@ -537,8 +536,17 @@
         gather_wait(m_all, m_recv, 2 * (CHIPS - 2), inner)
         gather_wait(g_all, g_recv, 2 * (CHIPS - 1), chip < CHIPS - 1)
         recurrence(m_all, g_all, f_out, f_all, f_send, f_recv, tuple(range(CHIPS)))
+        send_n(0, (0,))
         send_n(0, (1,))
         send_n(1, (0,))
+        send_n(1, (1,))
+
+    @pl.when(jnp.logical_not(is_solver))
+    def _():
+        send_n(0, (0,))
+        send_n(0, (1,))
+        send_n(1, (0,))
+        send_n(1, (1,))
 
 
     def landed_wait(landed, recv, rb):
@@ -571,12 +579,6 @@
 
         each_chip(backward_start, near_first=True, halves=(group,))
 
-    @pl.when(jnp.logical_not(is_solver))
-    def _():
-        send_n(0, (1,))
-        send_n(1, (0,))
-
-    send_n(1, (1,))
 
     out_copies = [
         pltpu.make_async_copy(res.at[:, mine], resid.at[:, :, half], out_sem.at[0]),
@@ -678,6 +680,27 @@
     for group in range(2):
         for copy in final(group):
             copy.wait()
+
+
+def hand_over(update, residual, update_out, residual_out, held, read, written):
+    pairs = [(0, update, update_out), (1, residual, residual_out)]
+    loads = [
+        pltpu.make_async_copy(src.at[ch], held.at[n, ch], read.at[n, ch])
+        for n, src, _ in pairs
+        for ch in range(5)
+    ]
+    stores = [
+        pltpu.make_async_copy(held.at[n, ch], dst.at[ch], written.at[n, ch])
+        for n, _, dst in pairs
+        for ch in range(5)
+    ]
+    for copy in loads:
+        copy.start()
+    for load, store in zip(loads, stores):
+        load.wait()
+        store.start()
+    for copy in stores:
+        copy.wait()
 
 
 def body(cons, phase, diag):
@@ -701,7 +724,7 @@
     out = jax.ShapeDtypeStruct(cons.shape, f32)
     anywhere = pl.BlockSpec(memory_space=pl.ANY)
     hbm = pl.BlockSpec(memory_space=pltpu.HBM)
-    return pl.pallas_call(
+    update, residual = pl.pallas_call(
         kernel,
         out_shape=(out, out),
         in_specs=[hbm] * 3,
@@ -712,6 +735,14 @@
         ),
         name="flow_sweep",
     )(cons, phase, diag)
+    return pl.pallas_call(
+        hand_over,
+        out_shape=(out, out),
+        in_specs=[hbm] * 2,
+        out_specs=(hbm, hbm),
+        scratch_shapes=[vm(2, *cons.shape), dma((2, 5)), dma((2, 5))],
+        name="hand_over",
+    )(update, residual)
 
 def solution(mesh):
     in_specs = (

time: 53.4 us -> 49.6 us (0.929)
  local copies, waits for them, and re-layouts: 3.93 us -> 0 us
    unnamed x2 -> x0, local copies, waits for them, and re-layouts: 3.93 us -> none
    pallas_call x0 -> x1, Pallas kernels: none -> 2.21 us  [body(): pl.pallas_call(hand_over, out_shape=(out, out), in_specs=[hbm] * 2, out_s...]
    pallas_call x1, Pallas kernels: 48.6 us -> 46.6 us  [body(): pl.pallas_call(kernel, out_shape=(out, out), in_specs=[hbm] * 3, out_spec...]
where the time goes in v3:
time: 49.6 us; the launch traced here: 49.5 us
  Pallas kernels  48.8 us (98%)
  between operations  0.64 us (1%)
    pallas_call x1, Pallas kernels, body(): pl.pallas_call(kernel, out_shape=(out, out), in_specs=[hbm] * 3, out_spec...  46.6 us
    pallas_call x1, Pallas kernels, body(): pl.pallas_call(hand_over, out_shape=(out, out), in_specs=[hbm] * 2, out_s...  2.21 us

profile of v3, /device:TPU:1, one launch (start us, length us, event | category | flops | bytes accessed | tf_op | source)
XLA Modules:
  0.0 49.5 jit_solution(4367191544829990094)
XLA Ops:
  0.6 46.6 %flow_sweep.1 = (f32[5,2,32,512]{3,2,1,0:T(8,128)}, f32[5,2,32,512]{3,2,1,0:T(8,128)}) custom-call(f32[5,2,32,512]{3,2,1,0:T(8,128)} %cons.1, s32[2,32,512]{2,1,0:T(8,128)} %phase.1, f32[5,5,2,32,512]{4,3,2,1,0:T(8,128)} %diag.1), custom_call_target="tpu_custom_call" | custom-call | tf_op jit(solution)/shard_map/flow_sweep/pallas_call | solution.py:727
  47.3 2.2 %hand_over.1 = (f32[5,2,32,512]{3,2,1,0:T(8,128)}, f32[5,2,32,512]{3,2,1,0:T(8,128)}) custom-call(f32[5,2,32,512]{3,2,1,0:T(8,128)} %get-tuple-element.4.update, f32[5,2,32,512]{3,2,1,0:T(8,128)} %get-tuple-element.5.residual), custom_call_target="tpu_custom_call" | custom-call | tf_op jit(solution)/shard_map/hand_over/pallas_call | solution.py:738

commit v4 on v3

--- a/solution.py
+++ b/solution.py
@@ -301,14 +301,10 @@
 
     swaps[2].start()
 
-    def send_n(half_at, quarters=(0, 1)):
-        def run(q, rb, lb):
-            chip_product(pn, 0, 1, n_out, q)
-            to_solver(q, n_out, n_all, n_send, n_recv)
-
+    def send_n():
         @pl.when(inner)
         def _():
-            each_chip(run, halves=(half_at,), quarters=quarters)
+            each_chip(lambda q, rb, lb: to_solver(q, n_out, n_all, n_send, n_recv))
 
     def set_primitives(plane, first):
         rows = pl.ds(aligned(first, 8), 8)
@@ -462,6 +458,7 @@
     @pl.when(inner)
     def _():
         nx_copy().wait_recv()
+        each_chip(lambda q, rb, lb: chip_product(pn, 0, 1, n_out, q))
 
 
     def response(q, rb, lb):
@@ -536,17 +533,11 @@
         gather_wait(m_all, m_recv, 2 * (CHIPS - 2), inner)
         gather_wait(g_all, g_recv, 2 * (CHIPS - 1), chip < CHIPS - 1)
         recurrence(m_all, g_all, f_out, f_all, f_send, f_recv, tuple(range(CHIPS)))
-        send_n(0, (0,))
-        send_n(0, (1,))
-        send_n(1, (0,))
-        send_n(1, (1,))
+        send_n()
 
     @pl.when(jnp.logical_not(is_solver))
     def _():
-        send_n(0, (0,))
-        send_n(0, (1,))
-        send_n(1, (0,))
-        send_n(1, (1,))
+        send_n()
 
 
     def landed_wait(landed, recv, rb):
@@ -579,13 +570,6 @@
 
         each_chip(backward_start, near_first=True, halves=(group,))
 
-
-    out_copies = [
-        pltpu.make_async_copy(res.at[:, mine], resid.at[:, :, half], out_sem.at[0]),
-        remote(res.at[:, theirs], resid.at[:, :, half], out_send.at[0], out_recv.at[0], peer),
-    ]
-    for copy in out_copies:
-        copy.start()
 
     def both_sweeps(q, rb, lb):
         flow = [f_all[q, ch] for ch in range(5)]
@@ -610,6 +594,13 @@
         gather_wait(n_all, n_recv, 2 * (CHIPS - 2), inner)
         gather_wait(h_all, h_recv, 2 * (CHIPS - 1), chip > 0)
         recurrence(n_all, h_all, w_out, w_all, w_send, w_recv, tuple(range(CHIPS - 1, -1, -1)))
+
+    out_copies = [
+        pltpu.make_async_copy(res.at[:, mine], resid.at[:, :, half], out_sem.at[0]),
+        remote(res.at[:, theirs], resid.at[:, :, half], out_send.at[0], out_recv.at[0], peer),
+    ]
+    for copy in out_copies:
+        copy.start()
 
     @pl.when(chip == CHIPS - 1)
     def _():

time: 49.6 us -> 49.6 us (level)
  no operation moved by 1% of the time
where the time goes in v4:
time: 49.6 us; the launch traced here: 49.5 us
  Pallas kernels  48.8 us (98%)
  between operations  0.64 us (1%)
    pallas_call x1, Pallas kernels, body(): pl.pallas_call(kernel, out_shape=(out, out), in_specs=[hbm] * 3, out_spec...  46.6 us
    pallas_call x1, Pallas kernels, body(): pl.pallas_call(hand_over, out_shape=(out, out), in_specs=[hbm] * 2, out_s...  2.21 us

profile of v4, /device:TPU:1, one launch (start us, length us, event | category | flops | bytes accessed | tf_op | source)
XLA Modules:
  0.0 49.5 jit_solution(9849253860782799125)
XLA Ops:
  0.6 46.6 %flow_sweep.1 = (f32[5,2,32,512]{3,2,1,0:T(8,128)}, f32[5,2,32,512]{3,2,1,0:T(8,128)}) custom-call(f32[5,2,32,512]{3,2,1,0:T(8,128)} %cons.1, s32[2,32,512]{2,1,0:T(8,128)} %phase.1, f32[5,5,2,32,512]{4,3,2,1,0:T(8,128)} %diag.1), custom_call_target="tpu_custom_call" | custom-call | tf_op jit(solution)/shard_map/flow_sweep/pallas_call | solution.py:718
  47.3 2.2 %hand_over.1 = (f32[5,2,32,512]{3,2,1,0:T(8,128)}, f32[5,2,32,512]{3,2,1,0:T(8,128)}) custom-call(f32[5,2,32,512]{3,2,1,0:T(8,128)} %get-tuple-element.4.update, f32[5,2,32,512]{3,2,1,0:T(8,128)} %get-tuple-element.5.residual), custom_call_target="tpu_custom_call" | custom-call | tf_op jit(solution)/shard_map/hand_over/pallas_call | solution.py:729
